TPU v7x, 32 devices: a whole 2x2x4 slice. The times are simulated.
32 devices in a mesh: ctx: 8 (over z, core), exp: 4 (over y, x).
Axes of the slice: x: 2, y: 2, z: 4, core: 2. Of those that a mesh axis runs over, the one named last changes fastest.
Arguments:
- queries: bfloat16 [4, 1024, 2048], P('exp', 'ctx'), may hold values from -18 to 18
- keys: bfloat16 [4, 1024, 2048], P('exp', 'ctx'), may hold values from -18 to 18
- values: bfloat16 [4, 1024, 2048], P('exp', 'ctx'), may hold values from -7 to 7
- segment_ids: int32 [4, 1024], P('exp', 'ctx'), may hold values from 0 to 2, never falling along the last dimension, each value on 1 to 512 neighbouring positions
- hidden_in: bfloat16 [4, 1024, 2048], P('exp', 'ctx'), may hold values from -6 to 6
- out_weight: bfloat16 [2048, 2048], replicated, may hold values from -0.125 to 0.125
- norm_gain: float32 [2048], replicated, may hold values from 0.25 to 1.75
- expert_ids: int32 [4, 1024, 6], P('exp', 'ctx'), may hold values from 0 to 15, all different within a row; in each aligned block of 128 rows (0 to 127, 128 to 255, ..., all dimensions but the last counted through in order) at most 64 rows name the same one
- gate_codes: int32 [4, 1024, 6], P('exp', 'ctx'), may hold values from 1 to 64
- w_in: bfloat16 [32, 2048, 1408], P(('ctx', 'exp')), may hold values from -0.125 to 0.125
- w_down: bfloat16 [32, 704, 2048], P(('ctx', 'exp')), may hold values from -0.15625 to 0.15625
Outputs:
- layer_out: bfloat16 [4, 1024, 2048], P('exp', 'ctx')
Inputs may be any that keep to these rules, and one draw needn't show every extreme that they name: `segment_ids`: segment numbers never fall along a stream; every segment has at most 512 positions and some segment of each stream has exactly 512. `expert_ids`: each token names 6 different experts; among the tokens of one device no expert is named more than 64 times, and some device reaches 64.
All inputs are finite; a program needn't handle non-finite values.
Results may differ from a plain program's by a relative error of at most 0.0095.
Values may be sent and summed in bfloat16 or wider, within the bound.
A program may use at most 128 MiB of HBM per device.

v0:
```python
import jax
import jax.numpy as jnp
from jax import lax
from jax.sharding import PartitionSpec as P

D = 2048
HEADS = 16
HEAD_DIM = 128
TOPK = 6


NEG_FILL = -1e30


def shifted(block, axis, distance):
    devices = range(lax.axis_size(axis))
    route = [(i - distance, i) for i in devices if i - distance in devices]
    return lax.ppermute(block, axis, route)


def attend_piece(state, piece, start, query_heads, query_pos, query_seg):
    run_top, run_sum, run_acc = state
    key_part, value_part, seg_part = piece
    width_rows = key_part.shape[1]
    key_heads = key_part[0].reshape(width_rows, HEADS, HEAD_DIM)
    value_heads = value_part[0].reshape(width_rows, HEADS, HEAD_DIM)
    key_pos = start + jnp.arange(width_rows, dtype=jnp.int32)
    key_seg = seg_part[0].astype(jnp.int32)
    allowed = (
        (key_pos[None, :] <= query_pos[:, None])
        & (key_pos[None, :] >= 0)
        & (key_seg[None, :] == query_seg[:, None])
    )
    scores = jnp.einsum(
        "qhd,khd->hqk", query_heads, key_heads, preferred_element_type=jnp.float32
    ) * HEAD_DIM ** (-0.5)
    scores = jnp.where(allowed[None], scores, NEG_FILL)
    new_top = jnp.maximum(run_top, jnp.max(scores, axis=-1))
    probs = jnp.where(allowed[None], jnp.exp(scores - new_top[:, :, None]), 0.0)
    rescale = jnp.exp(run_top - new_top)
    run_sum = run_sum * rescale + jnp.sum(probs, axis=-1)
    weighted = jnp.einsum(
        "hqk,khd->qhd", probs.astype(jnp.bfloat16), value_heads, preferred_element_type=jnp.float32
    )
    run_acc = run_acc * rescale.T[:, :, None] + weighted
    return (new_top, run_sum, run_acc)


def local(
    queries,
    keys,
    values,
    segment_ids,
    hidden_in,
    out_weight,
    norm_gain,
    expert_ids,
    gate_codes,
    w_in,
    w_down,
):
    rows = queries.shape[1]
    ctx_size = lax.axis_size("ctx")
    exp_size = lax.axis_size("exp")
    owners = ctx_size * exp_size
    experts = owners // 2
    capacity = rows * TOPK * 4 // (3 * experts)
    ctx_pos = lax.axis_index("ctx")
    query_pos = ctx_pos * rows + jnp.arange(rows, dtype=jnp.int32)
    query_heads = queries[0].reshape(rows, HEADS, HEAD_DIM)
    query_seg = segment_ids[0]
    seg_wire = segment_ids.astype(jnp.bfloat16)
    start_state = (
        jnp.full((HEADS, rows), NEG_FILL, jnp.float32),
        jnp.zeros((HEADS, rows), jnp.float32),
        jnp.zeros((rows, HEADS, HEAD_DIM), jnp.float32),
    )

    def fold_piece(state, piece, start):
        return attend_piece(state, piece, start, query_heads, query_pos, query_seg)

    own_state = fold_piece(start_state, (keys, values, seg_wire), ctx_pos * rows)

    def carry_step(step_index, carried):
        state, piece = carried
        piece = shifted((piece[0], piece[1], piece[2]), "ctx", 1)
        state = fold_piece(state, piece, (ctx_pos - step_index - 1) * rows)
        return (state, piece)

    final_state, leftover = lax.fori_loop(
        0, ctx_size // 2, carry_step, (own_state, (keys, values, seg_wire))
    )
    run_top, run_sum, run_acc = final_state
    attended = (run_acc / run_sum.T[:, :, None]).reshape(rows, D).astype(jnp.bfloat16)
    projected = jnp.dot(attended, out_weight, preferred_element_type=jnp.float32)
    mixed_wide = (
        (hidden_in[0].astype(jnp.float32) + projected).astype(jnp.bfloat16).astype(jnp.float32)
    )
    normed = (
        mixed_wide
        * lax.rsqrt(jnp.mean(mixed_wide * mixed_wide, axis=-1, keepdims=True) + 1e-06)
        * norm_gain
    ).astype(jnp.bfloat16)
    flat_ids = expert_ids[0].reshape(rows * TOPK)
    onehot = (flat_ids[:, None] == jnp.arange(experts, dtype=jnp.int32)[None, :]).astype(jnp.int32)
    slots = jnp.sum(jnp.cumsum(onehot, axis=0) * onehot, axis=1) - 1
    token_index = jnp.arange(rows * TOPK, dtype=jnp.int32) // TOPK
    send_buffer = (
        jnp.zeros((experts, capacity, D), jnp.bfloat16).at[flat_ids, slots].set(normed[token_index])
    )
    send_owners = jnp.broadcast_to(send_buffer[:, None], (experts, 2, capacity, D)).reshape(
        owners, capacity, D
    )
    gate_up = w_in[0]
    down_rows = w_down[0]
    half_units = down_rows.shape[0]
    inner = jnp.einsum(
        "scd,df->scf",
        lax.all_to_all(send_owners, ("ctx", "exp"), split_axis=0, concat_axis=0, tiled=True),
        gate_up,
        preferred_element_type=jnp.float32,
    )
    act = (jax.nn.silu(inner[..., :half_units]) * inner[..., half_units:]).astype(jnp.bfloat16)
    partial_out = jnp.einsum(
        "scf,fd->scd", act, down_rows, preferred_element_type=jnp.float32
    ).astype(jnp.bfloat16)
    returned = lax.all_to_all(partial_out, ("ctx", "exp"), split_axis=0, concat_axis=0, tiled=True)
    paired = returned.reshape(experts, 2, capacity, D)
    expert_out = paired[:, 0].astype(jnp.float32) + paired[:, 1].astype(jnp.float32)
    picked = expert_out[flat_ids, slots].reshape(rows, TOPK, D)
    codes = gate_codes[0].astype(jnp.float32)
    route_weight = codes / jnp.sum(codes, axis=-1, keepdims=True)
    routed = jnp.sum(route_weight[:, :, None] * picked, axis=1)
    layer_out = (mixed_wide + routed).astype(jnp.bfloat16)
    return layer_out[None]


def solution(mesh):
    placed = (
        P("exp", "ctx", None),
        P("exp", "ctx", None),
        P("exp", "ctx", None),
        P("exp", "ctx"),
        P("exp", "ctx", None),
        P(),
        P(),
        P("exp", "ctx", None),
        P("exp", "ctx", None),
        P(("ctx", "exp"), None, None),
        P(("ctx", "exp"), None, None),
    )
    return jax.shard_map(
        local, mesh=mesh, in_specs=placed, out_specs=P("exp", "ctx", None), check_vma=False
    )
```

profile of v0, /device:TPU:0, one launch (start us, length us, event | category | flops | bytes accessed | tf_op | source)
XLA Modules:
  0.0 723.7 jit_solution(11706366800797526471)
XLA Ops:
  2.1 2.0 copy.22
  4.2 2.0 copy.27
  6.2 2.0 copy.47
  8.2 2.0 copy.29
  11.0 1.5 fusion.44
  15.6 2.9 fusion.20
  18.6 88.0 %while.26 = (s32[]{:T(128)}, f32[16,128]{1,0:T(8,128)S(1)}, f32[16,128]{1,0:T(8,128)S(1)}, f32[128,16,128]{2,0,1:T(8,128)}, bf16[1,128,2048]{1,2,0:T(8,128)(2,1)...) while((s32[]{:T(128)}, f32[16,128]{1,0:T(8,128)S(1)}, ...), condition=%wide.region_5.6_spmd.clone, body=%wide.region_2.5_spmd.clone.sunk | while | flops 137173632 | bytes 13309741 | solution.py:90
  18.6 2.4 collective-permute-start.1
  21.0 5.4 collective-permute-start
  26.4 1.3 collective-permute-start.2
  27.9 1.7 fusion.64
  29.9 2.8 fusion.67
  32.7 1.9 copy.75
  35.4 9.6 %collective-permute-start.1 = (bf16[1,128]{1,0:T(2,128)(2,1)S(1)}, bf16[1,128]{1,0:T(2,128)(2,1)S(1)}, u32[]{:S(2)}, u32[]{:S(2)}) collective-permute-start(bf16[1,128]{1,0:T(2,128)(2,1)S(1)} %get-tuple-element.447), channel_id=1, source_target_pairs={{0,4},{4,8},{8,12},{12,16},{16,20},{20,24},{24,28},{1,5},{5,9},{9,... | collective-permute-start | bytes 776 | tf_op jit(solution)/shard_map/while/body/eval_jaxpr/ppermute | solution.py:18
  45.0 5.1 collective-permute-start
  50.1 1.3 collective-permute-start.2
  51.6 1.7 fusion.64
  53.6 2.8 fusion.67
  56.4 1.9 copy.75
  59.1 9.6 %collective-permute-start.1 = (bf16[1,128]{1,0:T(2,128)(2,1)S(1)}, bf16[1,128]{1,0:T(2,128)(2,1)S(1)}, u32[]{:S(2)}, u32[]{:S(2)}) collective-permute-start(bf16[1,128]{1,0:T(2,128)(2,1)S(1)} %get-tuple-element.447), channel_id=1, source_target_pairs={{0,4},{4,8},{8,12},{12,16},{16,20},{20,24},{24,28},{1,5},{5,9},{9,... | collective-permute-start | bytes 776 | tf_op jit(solution)/shard_map/while/body/eval_jaxpr/ppermute | solution.py:18
  68.7 5.1 collective-permute-start
  73.8 1.3 collective-permute-start.2
  75.4 1.7 fusion.64
  77.4 2.8 fusion.67
  80.2 1.9 copy.75
  82.8 9.6 %collective-permute-start.1 = (bf16[1,128]{1,0:T(2,128)(2,1)S(1)}, bf16[1,128]{1,0:T(2,128)(2,1)S(1)}, u32[]{:S(2)}, u32[]{:S(2)}) collective-permute-start(bf16[1,128]{1,0:T(2,128)(2,1)S(1)} %get-tuple-element.447), channel_id=1, source_target_pairs={{0,4},{4,8},{8,12},{12,16},{16,20},{20,24},{24,28},{1,5},{5,9},{9,... | collective-permute-start | bytes 776 | tf_op jit(solution)/shard_map/while/body/eval_jaxpr/ppermute | solution.py:18
  92.5 5.1 collective-permute-start
  99.1 1.7 fusion.64
  101.1 2.8 fusion.67
  103.9 1.9 copy.75
  106.6 2.5 copy.30
  109.1 1.3 divide_convert_fusion
  110.5 5.7 multiply_reduce_fusion.1
  116.2 1.7 reduce-window.6
  118.3 1.4 multiply_convert_fusion
  119.7 4.3 gather_fusion
  124.1 2.5 broadcast_in_dim.123
  126.6 137.5 %scatter_fusion = bf16[16,64,2048]{2,1,0:T(8,128)(2,1)} fusion(bf16[16,64,2048]{2,1,0:T(8,128)(2,1)} %broadcast_in_dim.123, s32[768]{0:T(1024)S(1)} %get-tuple-element.309, bf16[768,2048]{1,0:T(8,128)(2,1)} %gather_fusion), kind=kCustom, calls=%fused_computation.2 | custom fusion | bytes 9443328 | tf_op jit(solution)/shard_map/scatter | solution.py:109
  264.1 7.0 broadcast_in_dim.124
  271.1 198.2 %all_to_all.10 = bf16[32,64,2048]{2,1,0:T(8,128)(2,1)S(1)} all-to-all(bf16[32,64,2048]{2,1,0:T(8,128)(2,1)} %bitcast.100), channel_id=1, replica_groups=mesh['ctx'=8,'exp'=4] {'ctx','exp'}, dimensions={0} | all-to-all | bytes 16777216 | tf_op jit(solution)/shard_map/all_to_all | solution.py:119
  469.2 13.5 %fusion.13 = f32[32,64,1408]{2,1,0:T(8,128)S(1)} fusion(bf16[32,64,2048]{2,1,0:T(8,128)(2,1)S(1)} %all_to_all.10, bf16[1,2048,1408]{2,1,0:T(8,128)(2,1)S(1)} %bitcast.113), kind=kOutput, calls=%fused_computation.27 | convolution fusion | flops 11811160064 | bytes 25690112 | tf_op jit(solution)/shard_map/scd,df->scf/dot_general | solution.py:117
  482.8 9.5 %convolution_convert_fusion = bf16[32,64,2048]{2,1,0:T(8,128)(2,1)} fusion(f32[32,64,1408]{2,1,0:T(8,128)S(1)} %fusion.13, bf16[1,704,2048]{2,1,0:T(8,128)(2,1)S(1)} %copy-done), kind=kOutput, calls=%fused_computation.29 | convolution fusion | flops 5918425088 | bytes 23855104 | tf_op jit(solution)/shard_map/scf,fd->scd/dot_general | solution.py:124
  492.2 3.8 all-to-all-start.1
  496.3 188.1 %all-to-all-done.1 = bf16[32,64,2048]{2,1,0:T(8,128)(2,1)} async-done(((bf16[32,64,2048]{2,1,0:T(8,128)(2,1)}), bf16[32,64,2048]{2,1,0:T(8,128)(2,1)}, u32[]{:S(2)}, u32[]{:S(2)}) %all-to-all-start.1) | async-done | bytes 8388640 | tf_op jit(solution)/shard_map/all_to_all | solution.py:127
  684.4 8.7 %add_bitcast_fusion = f32[16,64,2048]{2,1,0:T(8,128)} fusion(bf16[16,2,64,2048]{3,2,1,0:T(8,128)(2,1)} %bitcast.14), kind=kLoop, calls=%fused_computation.24 | loop fusion | flops 6291456 | bytes 16777216 | tf_op jit(solution)/shard_map/add | solution.py:129
  693.1 15.2 %gather_fusion.1 = f32[768,2048]{1,0:T(8,128)} fusion(f32[16,64,2048]{2,1,0:T(8,128)} %add_bitcast_fusion, s32[768]{0:T(1024)S(1)} %get-tuple-element.308), kind=kCustom, calls=%fused_computation.1 | custom fusion | bytes 12589056 | tf_op jit(solution)/shard_map/gather | solution.py:130
  708.2 7.8 %reshape.349 = f32[128,6,2048]{2,1,0:T(8,128)} reshape(f32[768,2048]{1,0:T(8,128)} %gather_fusion.1) | data formatting | bytes 12582912 | tf_op jit(solution)/shard_map/reshape | solution.py:130
  716.1 6.7 multiply_reduce_fusion
  (99 shorter events, 13.5 us)
Async XLA Ops:
  0.0 482.7 %copy-start = (bf16[1,704,2048]{2,1,0:T(8,128)(2,1)S(1)}, bf16[1,704,2048]{2,1,0:T(8,128)(2,1)}, u32[]{:S(2)}) copy-start(bf16[1,704,2048]{2,1,0:T(8,128)(2,1)} %param.23) | copy-start | bytes 8650756
  0.0 18.6 %copy-start.4 = (s32[1,128]{1,0:T(1,128)S(1)}, s32[1,128]{1,0:T(1,128)}, u32[]{:S(2)}) copy-start(s32[1,128]{1,0:T(1,128)} %param.16) | copy-start | bytes 1540
  0.0 13.7 %copy-start.3 = (bf16[1,128,2048]{2,1,0:T(8,128)(2,1)S(1)}, bf16[1,128,2048]{2,1,0:T(8,128)(2,1)}, u32[]{:S(2)}) copy-start(bf16[1,128,2048]{2,1,0:T(8,128)(2,1)} %param.15) | copy-start | bytes 1572868
  12.5 1.0 copy-start.2
  18.6 9.1 %collective-permute-start.1 = (bf16[1,128]{1,0:T(2,128)(2,1)S(1)}, bf16[1,128]{1,0:T(2,128)(2,1)S(1)}, u32[]{:S(2)}, u32[]{:S(2)}) collective-permute-start(bf16[1,128]{1,0:T(2,128)(2,1)S(1)} %get-tuple-element.447), channel_id=1, source_target_pairs={{0,4},{4,8},{8,12},{12,16},{16,20},{20,24},{24,28},{1,5},{5,9},{9,... | collective-permute-start | bytes 776 | tf_op jit(solution)/shard_map/while/body/eval_jaxpr/ppermute | solution.py:18
  21.0 6.9 collective-permute-start
  26.4 3.5 collective-permute-start.2
  35.4 16.1 %collective-permute-start.1 = (bf16[1,128]{1,0:T(2,128)(2,1)S(1)}, bf16[1,128]{1,0:T(2,128)(2,1)S(1)}, u32[]{:S(2)}, u32[]{:S(2)}) collective-permute-start(bf16[1,128]{1,0:T(2,128)(2,1)S(1)} %get-tuple-element.447), channel_id=1, source_target_pairs={{0,4},{4,8},{8,12},{12,16},{16,20},{20,24},{24,28},{1,5},{5,9},{9,... | collective-permute-start | bytes 776 | tf_op jit(solution)/shard_map/while/body/eval_jaxpr/ppermute | solution.py:18
  45.0 6.6 collective-permute-start
  50.1 3.5 collective-permute-start.2
  59.1 16.1 %collective-permute-start.1 = (bf16[1,128]{1,0:T(2,128)(2,1)S(1)}, bf16[1,128]{1,0:T(2,128)(2,1)S(1)}, u32[]{:S(2)}, u32[]{:S(2)}) collective-permute-start(bf16[1,128]{1,0:T(2,128)(2,1)S(1)} %get-tuple-element.447), channel_id=1, source_target_pairs={{0,4},{4,8},{8,12},{12,16},{16,20},{20,24},{24,28},{1,5},{5,9},{9,... | collective-permute-start | bytes 776 | tf_op jit(solution)/shard_map/while/body/eval_jaxpr/ppermute | solution.py:18
  68.7 6.6 collective-permute-start
  73.8 3.5 collective-permute-start.2
  82.8 16.1 %collective-permute-start.1 = (bf16[1,128]{1,0:T(2,128)(2,1)S(1)}, bf16[1,128]{1,0:T(2,128)(2,1)S(1)}, u32[]{:S(2)}, u32[]{:S(2)}) collective-permute-start(bf16[1,128]{1,0:T(2,128)(2,1)S(1)} %get-tuple-element.447), channel_id=1, source_target_pairs={{0,4},{4,8},{8,12},{12,16},{16,20},{20,24},{24,28},{1,5},{5,9},{9,... | collective-permute-start | bytes 776 | tf_op jit(solution)/shard_map/while/body/eval_jaxpr/ppermute | solution.py:18
  92.5 6.6 collective-permute-start
  97.6 3.5 collective-permute-start.2
  110.5 7.9 %copy-start.6 = (f32[2048]{0:T(1024)S(1)}, f32[2048]{0:T(1024)}, u32[]{:S(2)}) copy-start(f32[2048]{0:T(1024)} %param.19) | copy-start | bytes 24580
  264.1 205.1 %slice-start = ((s8[5767168]{0:T(1024)(128)(4,1)}), s8[1572864]{0:T(1024)(128)(4,1)S(1)}, s32[]{:S(2)}) async-start(s8[5767168]{0:T(1024)(128)(4,1)} %bitcast.112), calls=%async_computation.2 | async-start | bytes 3145728
  271.1 198.2 %slice-start.1 = ((s8[5767168]{0:T(1024)(128)(4,1)}), s8[4194304]{0:T(1024)(128)(4,1)S(1)}, s32[]{:S(2)}) async-start(s8[5767168]{0:T(1024)(128)(4,1)} %bitcast.112), calls=%async_computation.3 | async-start | bytes 8388608
  492.2 3.8 copy-start.5
  492.2 192.1 %all-to-all-start.1 = ((bf16[32,64,2048]{2,1,0:T(8,128)(2,1)}), bf16[32,64,2048]{2,1,0:T(8,128)(2,1)}, u32[]{:S(2)}, u32[]{:S(2)}) async-start(bf16[32,64,2048]{2,1,0:T(8,128)(2,1)} %convolution_convert_fusion), calls=%async_computation.1 | async-start | bytes 16777216 | tf_op jit(solution)/shard_map/all_to_all | solution.py:127
  716.1 6.7 copy-start.1
where the time goes:
time: 728 us; the launch traced here: 724 us
  local copies, waits for them, and re-layouts  200 us (27%)
  blocking collectives  198 us (27%)
  waiting for transfers between devices  188 us (26%)
  starting transfers between devices  61 us (8%)
  matrix products  51.3 us (7%)
  other arithmetic  24.1 us (3%)
    all_to_all x1, blocking collectives, local(): lax.all_to_all(send_owners, ('ctx', 'exp'), split_axis=0, concat_axis=0,...  198 us
    all_to_all x1, waiting for transfers between devices, local(): lax.all_to_all(partial_out, ('ctx', 'exp'), split_axis=0, concat_axis=0,...  188 us
    scatter x1, local copies, waits for them, and re-layouts, local(): jnp.zeros((experts, capacity, D), jnp.bfloat16).at[flat_ids, slots]  138 us
    ppermute x12, starting transfers between devices, shifted(): return lax.ppermute(block, axis, route)  57.2 us
    gather x1, local copies, waits for them, and re-layouts, local(): picked = expert_out[flat_ids, slots].reshape(rows, TOPK, D)  15.2 us
  transfers between devices with their start and end apart: 13, of which 1 were waited for; matrix products, arithmetic and copies ran while one was open for 1% of the time, Pallas kernels for 0%

commit v1 on v0

v1 whole, which is shorter than its diff:
```python
import functools

import jax
import jax.numpy as jnp
from jax import lax
from jax.experimental import pallas as pl
from jax.experimental.pallas import tpu as pltpu
from jax.sharding import PartitionSpec as P

D = 2048
HEADS = 16
HEAD_DIM = 128
TOPK = 6
CHUNKS = 2
GROUP = 4

NEG_FILL = -1e30
BOTH = ("ctx", "exp")


def hop(block):
    devices = range(lax.axis_size("ctx"))
    return lax.ppermute(block, "ctx", [(i, i + 2) for i in devices if i + 2 in devices])


def swap(block):
    devices = range(lax.axis_size("ctx"))
    return lax.ppermute(block, "ctx", [(i, i ^ 1) for i in devices])


def attend_kernel(count, mask_ref, q_ref, *refs):
    k_refs, v_refs, out_ref = refs[:count], refs[count : 2 * count], refs[2 * count]
    allowed = mask_ref[...] > 0.0
    for head in range(GROUP):
        cols = slice(head * HEAD_DIM, (head + 1) * HEAD_DIM)
        query = q_ref[:, cols]
        scores = jnp.concatenate(
            [
                lax.dot_general(
                    query, k[:, cols], (((1,), (1,)), ((), ())), preferred_element_type=jnp.float32
                )
                for k in k_refs
            ],
            axis=1,
        ) * HEAD_DIM ** (-0.5)
        scores = jnp.where(allowed, scores, NEG_FILL)
        top = jnp.max(scores, axis=1, keepdims=True)
        probs = jnp.where(allowed, jnp.exp(scores - top), 0.0)
        total = jnp.sum(probs, axis=1, keepdims=True)
        low = probs.astype(jnp.bfloat16)
        rows = k_refs[0].shape[0]
        acc = sum(
            jnp.dot(
                low[:, i * rows : (i + 1) * rows], v[:, cols], preferred_element_type=jnp.float32
            )
            for i, v in enumerate(v_refs)
        )
        out_ref[:, cols] = (acc / total).astype(jnp.bfloat16)


def attend(mask, query, key_blocks, value_blocks):
    rows, width = query.shape
    count = len(key_blocks)
    wide = GROUP * HEAD_DIM
    block = pl.BlockSpec((rows, wide), lambda i: (0, i))
    return pl.pallas_call(
        functools.partial(attend_kernel, count),
        grid=(width // wide,),
        in_specs=[pl.BlockSpec(mask.shape, lambda i: (0, 0))] + [block] * (1 + 2 * count),
        out_specs=block,
        out_shape=jax.ShapeDtypeStruct((rows, width), jnp.bfloat16),
        compiler_params=pltpu.CompilerParams(vmem_limit_bytes=32 * 1024 * 1024),
        cost_estimate=pl.CostEstimate(
            flops=4 * rows * rows * count * width,
            bytes_accessed=4 * rows * width * (count + 1),
            transcendentals=rows * rows * count * HEADS,
        ),
    )(mask, query, *key_blocks, *value_blocks)


def gather_blocks(block):
    steps = lax.axis_size("ctx") // 4
    first = lax.axis_index("ctx") % 2 == 0
    chain = [block]
    for _ in range(steps):
        chain.append(hop(chain[-1]))
    others = [swap(chain[k]) for k in range(1, steps)]
    return chain + others + [swap(jnp.where(first, chain[0], chain[-1]))]


def expert_half(tokens, gate_up, down_rows):
    half = down_rows.shape[0]
    inner = jnp.dot(tokens, gate_up, preferred_element_type=jnp.float32)
    act = (jax.nn.silu(inner[:, :half]) * inner[:, half:]).astype(jnp.bfloat16)
    return jnp.dot(act, down_rows, preferred_element_type=jnp.float32)


def earlier(rows):
    order = jnp.arange(rows)
    return (order[:, None] < order[None, :]).astype(jnp.bfloat16)


def routed_by_gather(normed, meta, w_in, w_down):
    rows = normed.shape[0]
    owners = meta.shape[0]
    owner = lax.axis_index("ctx") * lax.axis_size("exp") + lax.axis_index("exp")
    ids, codes = meta[:, :TOPK] // 128, (meta[:, :TOPK] % 128).astype(jnp.float32)
    hit = jnp.where(ids == owner // 2, codes, 0.0)
    weight = jnp.sum(hit, axis=1) / jnp.sum(codes, axis=1)
    part_rows = rows // CHUNKS
    pieces = []
    for c in range(CHUNKS):
        span = slice(c * part_rows, (c + 1) * part_rows)
        tokens = lax.all_gather(normed[span], BOTH, axis=0, tiled=True)
        part = expert_half(tokens, w_in, w_down)
        share = weight[:, span].reshape(owners * part_rows, 1)
        part = jnp.where(share > 0.0, part * share, 0.0).astype(jnp.bfloat16)
        pieces.append(lax.psum_scatter(part, BOTH, scatter_dimension=0, tiled=True))
    return jnp.concatenate(pieces, axis=0).astype(jnp.float32)


def routed_by_exchange(normed, ids, codes, capacity, w_in, w_down):
    rows = normed.shape[0]
    owners = lax.axis_size("ctx") * lax.axis_size("exp")
    experts = owners // 2
    codes = codes.astype(jnp.float32)
    route = codes / jnp.sum(codes, axis=1, keepdims=True)
    named = ids[:, :, None] == jnp.arange(experts, dtype=jnp.int32)
    member = jnp.any(named, axis=1)
    weight = jnp.sum(jnp.where(named, route[:, :, None], 0.0), axis=1)
    rank = jnp.einsum(
        "st,se->te", earlier(rows), member.astype(jnp.bfloat16), preferred_element_type=jnp.float32
    ).astype(jnp.int32)
    slot = jnp.where(member, rank, -1).T[:, None, :]
    chosen = slot == jnp.arange(capacity, dtype=jnp.int32)[None, :, None]
    sent = jnp.einsum(
        "ect,td->ecd", chosen.astype(jnp.bfloat16), normed, preferred_element_type=jnp.float32
    ).astype(jnp.bfloat16)
    sent = jnp.broadcast_to(sent[:, None], (experts, 2, capacity, D)).reshape(owners, capacity, D)
    got = lax.all_to_all(sent, BOTH, split_axis=0, concat_axis=0, tiled=True)
    part = expert_half(got.reshape(owners * capacity, D), w_in, w_down).astype(jnp.bfloat16)
    back = lax.all_to_all(
        part.reshape(owners, capacity, D), BOTH, split_axis=0, concat_axis=0, tiled=True
    ).reshape(experts, 2, capacity, D)
    expert_out = back[:, 0].astype(jnp.float32) + back[:, 1].astype(jnp.float32)
    spread = jnp.where(chosen, weight.T[:, None, :], 0.0)
    return jnp.einsum("ect,ecd->td", spread, expert_out, precision=lax.Precision.HIGHEST)


def local(
    queries,
    keys,
    values,
    segment_ids,
    hidden_in,
    out_weight,
    norm_gain,
    expert_ids,
    gate_codes,
    w_in,
    w_down,
):
    rows = queries.shape[1]
    ctx_size = lax.axis_size("ctx")
    exp_size = lax.axis_size("exp")
    owners = ctx_size * exp_size
    capacity = rows * TOPK * 8 // (3 * owners)
    me = lax.axis_index("ctx")
    packed = (expert_ids[0] * 128 + gate_codes[0]).T
    meta = lax.all_gather(
        jnp.concatenate([packed, segment_ids, segment_ids], axis=0), BOTH, axis=0, tiled=False
    )
    segs = lax.dynamic_index_in_dim(
        meta[:, TOPK].reshape(ctx_size, exp_size, rows), lax.axis_index("exp"), 1, keepdims=False
    )
    steps = ctx_size // 4
    other = me + 1 - 2 * (me % 2)
    whose = jnp.stack(
        [me - 2 * k for k in range(steps + 1)]
        + [other - 2 * k for k in range(1, steps)]
        + [jnp.where(me % 2 == 0, other - 2 * steps, other)]
    )
    key_pos = (whose[:, None] * rows + jnp.arange(rows, dtype=jnp.int32)).reshape(-1)
    key_seg = segs[jnp.maximum(whose, 0)].reshape(-1)
    query_pos = me * rows + jnp.arange(rows, dtype=jnp.int32)
    mask = (
        (key_pos[None, :] <= query_pos[:, None])
        & (key_pos[None, :] >= 0)
        & (key_seg[None, :] == segment_ids[0][:, None])
    ).astype(jnp.float32)
    attended = attend(mask, queries[0], gather_blocks(keys[0]), gather_blocks(values[0]))
    projected = jnp.dot(attended, out_weight, preferred_element_type=jnp.float32)
    mixed_wide = (
        (hidden_in[0].astype(jnp.float32) + projected).astype(jnp.bfloat16).astype(jnp.float32)
    )
    normed = (
        mixed_wide
        * lax.rsqrt(jnp.mean(mixed_wide * mixed_wide, axis=-1, keepdims=True) + 1e-06)
        * norm_gain
    ).astype(jnp.bfloat16)
    if 2 * capacity >= rows:
        routed = routed_by_gather(normed, meta, w_in[0], w_down[0])
    else:
        routed = routed_by_exchange(
            normed, expert_ids[0], gate_codes[0], capacity, w_in[0], w_down[0]
        )
    return (mixed_wide + routed).astype(jnp.bfloat16)[None]


def solution(mesh):
    placed = (
        P("exp", "ctx", None),
        P("exp", "ctx", None),
        P("exp", "ctx", None),
        P("exp", "ctx"),
        P("exp", "ctx", None),
        P(),
        P(),
        P("exp", "ctx", None),
        P("exp", "ctx", None),
        P(("ctx", "exp"), None, None),
        P(("ctx", "exp"), None, None),
    )
    return jax.shard_map(
        local, mesh=mesh, in_specs=placed, out_specs=P("exp", "ctx", None), check_vma=False
    )
```

time: 728 us -> 674 us (0.926)
  waiting for transfers between devices: 188 us -> 477 us
  local copies, waits for them, and re-layouts: 200 us -> 7.27 us
  blocking collectives: 198 us -> 79.5 us
  starting transfers between devices: 61 us -> 14.2 us
  other arithmetic: 24.1 us -> 7.89 us
  matrix products: 51.3 us -> 65.9 us
  between operations: 0.21 us -> 13.3 us
  Pallas kernels: 0 us -> 8.27 us
    reduce_scatter x0 -> x2, waiting for transfers between devices: none -> 341 us  [routed_by_gather(): pieces.append(lax.psum_scatter(part, BOTH, scatter_dimension=0, tiled=True))]
    all_to_all x1 -> x0, blocking collectives: 198 us -> none  [local(): lax.all_to_all(send_owners, ('ctx', 'exp'), split_axis=0, concat_axis=0,...]
    all_to_all x1 -> x0, waiting for transfers between devices: 188 us -> none  [local(): lax.all_to_all(partial_out, ('ctx', 'exp'), split_axis=0, concat_axis=0,...]
    scatter x1 -> x0, local copies, waits for them, and re-layouts: 138 us -> none  [local(): jnp.zeros((experts, capacity, D), jnp.bfloat16).at[flat_ids, slots]]
    all_gather x0 -> x2, waiting for transfers between devices: none -> 123 us  [routed_by_gather(): tokens = lax.all_gather(normed[span], BOTH, axis=0, tiled=True)]
    all_gather x0 -> x1, blocking collectives: none -> 79.5 us  [local(): lax.all_gather(jnp.concatenate([packed, segment_ids, segment_ids], axis=0...]
    ppermute x12 -> x8, starting transfers between devices: 57.2 us -> 13.6 us  [the longest x4 12.9 us: hop(): lax.ppermute(block, 'ctx', [(i, i + 2) for i in devices if i + 2 in devic...]
    gather x2 -> x1, local copies, waits for them, and re-layouts: 19.5 us -> 0.55 us  [local(): key_seg = segs[jnp.maximum(whose, 0)].reshape(-1)]
  transfers between devices with their start and end apart: 13 -> 12, of which waited for: 1 -> 7; matrix products, arithmetic and copies ran while one was open for 1% -> 10% of each run, Pallas kernels for 0% -> 0%
where the time goes in v1:
time: 674 us
  waiting for transfers between devices  477 us (71%)
  blocking collectives  79.5 us (12%)
  matrix products  65.9 us (10%)
  starting transfers between devices  14.2 us (2%)
  between operations  13.3 us (2%)
  Pallas kernels  8.27 us (1%)
  other arithmetic  7.89 us (1%)
  local copies, waits for them, and re-layouts  7.27 us (1%)
    reduce_scatter x2, waiting for transfers between devices, routed_by_gather(): pieces.append(lax.psum_scatter(part, BOTH, scatter_dimension=0, tiled=True))  341 us
    all_gather x2, waiting for transfers between devices, routed_by_gather(): tokens = lax.all_gather(normed[span], BOTH, axis=0, tiled=True)  123 us
    all_gather x1, blocking collectives, local(): lax.all_gather(jnp.concatenate([packed, segment_ids, segment_ids], axis=0...  79.5 us
    dot_general x2, matrix products, expert_half(): inner = jnp.dot(tokens, gate_up, preferred_element_type=jnp.float32)  37.4 us
    dot_general x2, matrix products, expert_half(): return jnp.dot(act, down_rows, preferred_element_type=jnp.float32)  23.7 us
  transfers between devices with their start and end apart: 12, of which 7 were waited for; matrix products, arithmetic and copies ran while one was open for 10% of the time, Pallas kernels for 0%

profile of v1, /device:TPU:0, one launch (start us, length us, event | category | flops | bytes accessed | tf_op | source)
XLA Modules:
  0.0 673.6 jit_solution(4708714237501410221)
XLA Ops:
  6.5 6.0 collective-permute-start
  12.5 3.5 collective-permute-start.4
  16.0 0.7 fusion.19
  16.7 0.7 pad_add_fusion
  17.5 79.5 %all-gather = s32[256,128]{1,0:T(8,128)S(1)} all-gather(s32[8,128]{1,0:T(8,128)S(1)} %pad_add_fusion), channel_id=2, replica_groups=mesh['ctx'=8,'exp'=4] {'ctx','exp'}, dimensions={0}, use_global_device_ids=true | all-gather | bytes 135168 | tf_op jit(solution)/shard_map/all_gather | solution.py:170
  97.0 0.6 slice.43
  97.6 0.1 stack.41
  97.7 0.1 stack.35
  97.8 1.3 collective-permute-start.1
  99.2 0.1 broadcast_compare_fusion.2
  99.3 2.1 collective-permute-start.5
  101.4 0.7 constant_dynamic-slice_fusion
  102.1 0.6 gather_fusion
  102.7 0.1 collective-permute-start.2
  102.8 0.5 collective-permute-start.6
  103.3 8.6 %collective-permute-done.1.refs_2_ = bf16[128,2048]{1,0:T(8,128)(2,1)S(1)} collective-permute-done((bf16[128,2048]{1,0:T(8,128)(2,1)}, bf16[128,2048]{1,0:T(8,128)(2,1)S(1)}, u32[]{:S(2)}, u32[]{:S(2)}) %collective-permute-start.1) | collective-permute-done | bytes 524320 | tf_op jit(solution)/shard_map/ppermute | solution.py:23
  111.8 1.1 broadcast_select_fusion.1
  112.9 0.1 collective-permute-start.3
  113.0 4.5 collective-permute-done.5.refs_7_
  117.5 1.1 broadcast_select_fusion
  118.6 0.1 collective-permute-start.7
  118.7 0.7 add_bitcast_fusion
  119.4 0.8 and_convert_fusion.mask_ref
  120.2 0.3 collective-permute-done.7.refs_9_
  120.5 1.0 copy-done.1
  121.6 1.0 copy-done.2
  122.6 1.0 copy-done.3
  123.7 8.3 %shard_map.109 = bf16[128,2048]{1,0:T(8,128)(2,1)S(1)} custom-call(f32[128,640]{1,0:T(8,128)S(1)} %and_convert_fusion.mask_ref, bf16[128,2048]{1,0:T(8,128)(2,1)S(1)} %bitcast.53, bf16[128,2048]{1,0:T(8,128)(2,1)S(1)} %bitcast.50, bf16[128,2048]{1,0:T(8,128)(2,1)} %collective-permute-done.refs_1_, bf16[128,2048]{1,0:T(8,128)(2,1)S(1)} %collective-permute-done.1.refs_2_, ...), custom_call_target="tpu_custom_call" | custom-call | flops 671088640 | bytes 6291456 | tf_op jit(solution)/shard_map/pallas_call | solution.py:66
  132.0 4.8 multiply_reduce_fusion
  136.8 1.0 copy-done.4
  137.8 0.2 multiply_convert_fusion
  137.9 0.8 fusion.22
  138.8 0.7 all-gather.4.cloned.1.call-update
  139.5 0.2 reduce-scatter.5.cloned.1.call-start
  139.8 0.2 fusion.18
  140.0 0.1 fusion.23
  140.1 0.1 reshape.183
  140.1 74.6 %all-gather.6.cloned.1.call-done = bf16[2048,2048]{1,0:T(8,128)(2,1)} async-done(((bf16[64,2048]{1,0:T(8,128)(2,1)}), bf16[2048,2048]{1,0:T(8,128)(2,1)}) %all-gather.6.cloned.1.call-update) | async-done | bytes 8388624 | tf_op jit(solution)/shard_map/all_gather | solution.py:114
  214.7 18.7 %fusion.2 = f32[2048,1408]{0,1:T(8,128)} fusion(bf16[2048,2048]{1,0:T(8,128)(2,1)} %all-gather.6.cloned.1.call-done, bf16[1,2048,1408]{2,1,0:T(8,128)(2,1)} %param.20), kind=kOutput, calls=%fused_computation.7 | convolution fusion | flops 11811160064 | bytes 25690112 | tf_op jit(solution)/shard_map/dot_general | solution.py:93
  233.4 11.9 %select_convert_fusion = bf16[2048,2048]{1,0:T(8,128)(2,1)} fusion(f32[2048]{0:T(1024)S(1)} %reshape.183, pred[2048]{0:T(1024)(128)(4,1)S(1)} %broadcast_compare_fusion, f32[2048,1408]{0,1:T(8,128)} %fusion.2, bf16[1,704,2048]{2,1,0:T(8,128)(2,1)S(1)} %copy-done), kind=kOutput, calls=%fused_computation.1 | convolution fusion | flops 5926813696 | bytes 22816768 | tf_op jit(solution)/shard_map/dot_general | solution.py:95
  245.4 0.3 reduce-scatter.3.cloned.1.call-start
  245.7 0.1 reshape.182
  245.7 48.1 %all-gather.4.cloned.1.call-done = bf16[2048,2048]{1,0:T(8,128)(2,1)} async-done(((bf16[64,2048]{1,0:T(8,128)(2,1)}), bf16[2048,2048]{1,0:T(8,128)(2,1)}) %all-gather.4.cloned.1.call-update) | async-done | bytes 8388624 | tf_op jit(solution)/shard_map/all_gather | solution.py:114
  293.8 18.7 %fusion.4 = f32[2048,1408]{0,1:T(8,128)} fusion(bf16[2048,2048]{1,0:T(8,128)(2,1)} %all-gather.4.cloned.1.call-done, bf16[1,2048,1408]{2,1,0:T(8,128)(2,1)} %param.20), kind=kOutput, calls=%fused_computation.9 | convolution fusion | flops 11811160064 | bytes 25690112 | tf_op jit(solution)/shard_map/dot_general | solution.py:93
  312.5 11.8 %select_convert_fusion.1 = bf16[2048,2048]{1,0:T(8,128)(2,1)} fusion(f32[2048]{0:T(1024)S(1)} %reshape.182, pred[2048]{0:T(1024)(128)(4,1)S(1)} %broadcast_compare_fusion.1, f32[2048,1408]{0,1:T(8,128)} %fusion.4, bf16[1,704,2048]{2,1,0:T(8,128)(2,1)S(1)} %copy-done), kind=kOutput, calls=%fused_computation.2 | convolution fusion | flops 5926813696 | bytes 22816768 | tf_op jit(solution)/shard_map/dot_general | solution.py:95
  324.3 153.9 %reduce-scatter.5.cloned.1.call-done = bf16[64,2048]{1,0:T(8,128)(2,1)} async-done(((bf16[2048,2048]{1,0:T(8,128)(2,1)}), bf16[64,2048]{1,0:T(8,128)(2,1)}) %reduce-scatter.5.cloned.1.call-update) | async-done | bytes 262160 | tf_op jit(solution)/shard_map/reduce_scatter | solution.py:118
  478.2 186.7 %reduce-scatter.3.cloned.1.call-done = bf16[64,2048]{1,0:T(8,128)(2,1)} async-done(((bf16[2048,2048]{1,0:T(8,128)(2,1)}), bf16[64,2048]{1,0:T(8,128)(2,1)}) %reduce-scatter.3.cloned.1.call-update) | async-done | bytes 262160 | tf_op jit(solution)/shard_map/reduce_scatter | solution.py:118
  664.9 2.2 fusion.14
  (30 shorter events, 0.2 us)
Async XLA Ops:
  6.5 226.9 %copy-start = (bf16[1,704,2048]{2,1,0:T(8,128)(2,1)S(1)}, bf16[1,704,2048]{2,1,0:T(8,128)(2,1)}, u32[]{:S(2)}) copy-start(bf16[1,704,2048]{2,1,0:T(8,128)(2,1)} %param.21) | copy-start | bytes 8650756
  6.5 208.2 %all-gather.6.cloned.1.call-start = ((), (), s32[]{:S(2)}) async-start(), calls=%async_computation.4 | async-start | bytes 8650752 | tf_op jit(solution)/shard_map/all_gather | solution.py:114
  6.5 91.3 %collective-permute-start = (bf16[128,2048]{1,0:T(8,128)(2,1)}, bf16[128,2048]{1,0:T(8,128)(2,1)}, u32[]{:S(2)}, u32[]{:S(2)}) collective-permute-start(bf16[128,2048]{1,0:T(8,128)(2,1)} %bitcast.49), channel_id=1, source_target_pairs={{0,8},{4,12},{8,16},{12,20},{16,24},{20,28},{1,9},{5,13},{9,17},{1... | collective-permute-start | bytes 1572872 | tf_op jit(solution)/shard_map/ppermute | solution.py:23
  12.5 86.7 %collective-permute-start.4 = (bf16[128,2048]{1,0:T(8,128)(2,1)}, bf16[128,2048]{1,0:T(8,128)(2,1)}, u32[]{:S(2)}, u32[]{:S(2)}) collective-permute-start(bf16[128,2048]{1,0:T(8,128)(2,1)} %bitcast.51), channel_id=1, source_target_pairs={{0,8},{4,12},{8,16},{12,20},{16,24},{20,28},{1,9},{5,13},{9,17},{1... | collective-permute-start | bytes 1572872 | tf_op jit(solution)/shard_map/ppermute | solution.py:23
  97.8 14.0 %collective-permute-start.1 = (bf16[128,2048]{1,0:T(8,128)(2,1)}, bf16[128,2048]{1,0:T(8,128)(2,1)S(1)}, u32[]{:S(2)}, u32[]{:S(2)}) collective-permute-start(bf16[128,2048]{1,0:T(8,128)(2,1)} %collective-permute-done.refs_1_), channel_id=1, source_target_pairs={{0,8},{4,12},{8,16},{12,20},{16,24},{20,28},{1,9},{5,13},{9,17},{1... | collective-permute-start | bytes 1572872 | tf_op jit(solution)/shard_map/ppermute | solution.py:23
  99.2 2.9 copy-start.7
  99.3 18.2 %collective-permute-start.5 = (bf16[128,2048]{1,0:T(8,128)(2,1)}, bf16[128,2048]{1,0:T(8,128)(2,1)}, u32[]{:S(2)}, u32[]{:S(2)}) collective-permute-start(bf16[128,2048]{1,0:T(8,128)(2,1)} %collective-permute-done.4.refs_6_), channel_id=1, source_target_pairs={{0,8},{4,12},{8,16},{12,20},{16,24},{20,28},{1,9},{5,13},{9,17},{1... | collective-permute-start | bytes 1572872 | tf_op jit(solution)/shard_map/ppermute | solution.py:23
  102.7 29.3 %copy-start.5 = (bf16[1,128,2048]{2,1,0:T(8,128)(2,1)S(1)}, bf16[1,128,2048]{2,1,0:T(8,128)(2,1)}, u32[]{:S(2)}) copy-start(bf16[1,128,2048]{2,1,0:T(8,128)(2,1)} %param.15) | copy-start | bytes 1572868
  102.7 17.5 %collective-permute-start.2 = (bf16[128,2048]{1,0:T(8,128)(2,1)}, bf16[128,2048]{1,0:T(8,128)(2,1)S(1)}, u32[]{:S(2)}, u32[]{:S(2)}) collective-permute-start(bf16[128,2048]{1,0:T(8,128)(2,1)} %collective-permute-done.refs_1_), channel_id=1, source_target_pairs={{0,4},{4,0},{8,12},{12,8},{16,20},{20,16},{24,28},{28,24},{1,5},{5... | collective-permute-start | bytes 1572872 | tf_op jit(solution)/shard_map/ppermute | solution.py:28
  102.8 17.4 %collective-permute-start.6 = (bf16[128,2048]{1,0:T(8,128)(2,1)}, bf16[128,2048]{1,0:T(8,128)(2,1)S(1)}, u32[]{:S(2)}, u32[]{:S(2)}) collective-permute-start(bf16[128,2048]{1,0:T(8,128)(2,1)} %collective-permute-done.4.refs_6_), channel_id=1, source_target_pairs={{0,4},{4,0},{8,12},{12,8},{16,20},{20,16},{24,28},{28,24},{1,5},{5... | collective-permute-start | bytes 1572872 | tf_op jit(solution)/shard_map/ppermute | solution.py:28
  112.9 7.3 %collective-permute-start.3 = (bf16[128,2048]{1,0:T(8,128)(2,1)S(1)}, bf16[128,2048]{1,0:T(8,128)(2,1)S(1)}, u32[]{:S(2)}, u32[]{:S(2)}) collective-permute-start(bf16[128,2048]{1,0:T(8,128)(2,1)S(1)} %broadcast_select_fusion.1), channel_id=1, source_target_pairs={{0,4},{4,0},{8,12},{12,8},{16,20},{20,16},{24,28},{28,24},{1,5},{5... | collective-permute-start | bytes 1572872 | tf_op jit(solution)/shard_map/ppermute | solution.py:28
  118.6 2.0 collective-permute-start.7
  120.5 1.0 copy-start.1
  121.6 1.0 copy-start.2
  122.6 1.0 copy-start.3
  131.9 5.8 copy-start.6
  136.8 1.0 copy-start.4
  138.8 155.0 %all-gather.4.cloned.1.call-start = ((), (), s32[]{:S(2)}) async-start(), calls=%async_computation.2 | async-start | bytes 8650752 | tf_op jit(solution)/shard_map/all_gather | solution.py:114
  139.5 338.7 %reduce-scatter.5.cloned.1.call-start = ((), (), s32[]{:S(2)}) async-start(), calls=%async_computation.5 | async-start | bytes 8650752 | tf_op jit(solution)/shard_map/reduce_scatter | solution.py:118
  245.4 419.5 %reduce-scatter.3.cloned.1.call-start = ((), (), s32[]{:S(2)}) async-start(), calls=%async_computation.3 | async-start | bytes 8650752 | tf_op jit(solution)/shard_map/reduce_scatter | solution.py:118
Sparse Core Ops, SparseCore 0:
  138.9 75.8 all-gather.5
  217.6 76.1 all-gather.3
  296.1 182.0 reduce-scatter.4
  480.3 184.4 reduce-scatter.2

commit v2 on v1

--- a/solution.py
+++ b/solution.py
@@ -100,22 +100,50 @@
     return (order[:, None] < order[None, :]).astype(jnp.bfloat16)
 
 
-def routed_by_gather(normed, meta, w_in, w_down):
+def halved_sum(part, order):
+    sizes = {"ctx": lax.axis_size("ctx"), "exp": lax.axis_size("exp")}
+    left = [
+        (axis, bit) for axis in BOTH for bit in reversed(range(sizes[axis].bit_length() - 1))
+    ]
+    block = part.reshape((2,) * len(left) + part.shape[1:])
+    for axis, bit in order:
+        place = left.index((axis, bit))
+        left.pop(place)
+        mine = (lax.axis_index(axis) >> bit) & 1
+        kept = lax.dynamic_index_in_dim(block, mine, place, keepdims=False)
+        sent = lax.dynamic_index_in_dim(block, 1 - mine, place, keepdims=False)
+        pairs = [(i, i ^ (1 << bit)) for i in range(sizes[axis])]
+        got = lax.ppermute(sent, axis, pairs)
+        block = (kept.astype(jnp.float32) + got.astype(jnp.float32)).astype(jnp.bfloat16)
+    return block
+
+
+def routed_by_gather(normed, ids, codes, w_in, w_down):
     rows = normed.shape[0]
-    owners = meta.shape[0]
+    owners = lax.axis_size("ctx") * lax.axis_size("exp")
     owner = lax.axis_index("ctx") * lax.axis_size("exp") + lax.axis_index("exp")
-    ids, codes = meta[:, :TOPK] // 128, (meta[:, :TOPK] % 128).astype(jnp.float32)
-    hit = jnp.where(ids == owner // 2, codes, 0.0)
-    weight = jnp.sum(hit, axis=1) / jnp.sum(codes, axis=1)
+    blank = jnp.zeros((rows, HEAD_DIM - 2 * TOPK), jnp.bfloat16)
+    wide = jnp.concatenate(
+        [normed, ids.astype(jnp.bfloat16), codes.astype(jnp.bfloat16), blank], axis=1
+    )
+    w_wide = jnp.concatenate([w_in, jnp.zeros((HEAD_DIM, w_in.shape[1]), w_in.dtype)], axis=0)
     part_rows = rows // CHUNKS
+    deep = [("ctx", bit) for bit in range(1, lax.axis_size("ctx").bit_length() - 1)]
+    flat = [("exp", bit) for bit in range(lax.axis_size("exp").bit_length() - 1)]
+    core = [("ctx", 0)]
+    orders = [core + flat + deep, core + deep + flat[::-1]]
     pieces = []
     for c in range(CHUNKS):
         span = slice(c * part_rows, (c + 1) * part_rows)
-        tokens = lax.all_gather(normed[span], BOTH, axis=0, tiled=True)
-        part = expert_half(tokens, w_in, w_down)
-        share = weight[:, span].reshape(owners * part_rows, 1)
+        tokens = lax.all_gather(wide[span], BOTH, axis=0, tiled=True)
+        named = tokens[:, D : D + TOPK].astype(jnp.int32) == owner // 2
+        code = tokens[:, D + TOPK : D + 2 * TOPK].astype(jnp.float32)
+        share = jnp.sum(jnp.where(named, code, 0.0), axis=1, keepdims=True) / jnp.sum(
+            code, axis=1, keepdims=True
+        )
+        part = expert_half(tokens, w_wide, w_down)
         part = jnp.where(share > 0.0, part * share, 0.0).astype(jnp.bfloat16)
-        pieces.append(lax.psum_scatter(part, BOTH, scatter_dimension=0, tiled=True))
+        pieces.append(halved_sum(part.reshape(owners, part_rows, D), orders[c % 2]))
     return jnp.concatenate(pieces, axis=0).astype(jnp.float32)
 
 
@@ -166,13 +194,6 @@
     owners = ctx_size * exp_size
     capacity = rows * TOPK * 8 // (3 * owners)
     me = lax.axis_index("ctx")
-    packed = (expert_ids[0] * 128 + gate_codes[0]).T
-    meta = lax.all_gather(
-        jnp.concatenate([packed, segment_ids, segment_ids], axis=0), BOTH, axis=0, tiled=False
-    )
-    segs = lax.dynamic_index_in_dim(
-        meta[:, TOPK].reshape(ctx_size, exp_size, rows), lax.axis_index("exp"), 1, keepdims=False
-    )
     steps = ctx_size // 4
     other = me + 1 - 2 * (me % 2)
     whose = jnp.stack(
@@ -181,7 +202,7 @@
         + [jnp.where(me % 2 == 0, other - 2 * steps, other)]
     )
     key_pos = (whose[:, None] * rows + jnp.arange(rows, dtype=jnp.int32)).reshape(-1)
-    key_seg = segs[jnp.maximum(whose, 0)].reshape(-1)
+    key_seg = jnp.concatenate(gather_blocks(segment_ids), axis=1)[0]
     query_pos = me * rows + jnp.arange(rows, dtype=jnp.int32)
     mask = (
         (key_pos[None, :] <= query_pos[:, None])
@@ -199,7 +220,7 @@
         * norm_gain
     ).astype(jnp.bfloat16)
     if 2 * capacity >= rows:
-        routed = routed_by_gather(normed, meta, w_in[0], w_down[0])
+        routed = routed_by_gather(normed, expert_ids[0], gate_codes[0], w_in[0], w_down[0])
     else:
         routed = routed_by_exchange(
             normed, expert_ids[0], gate_codes[0], capacity, w_in[0], w_down[0]

time: 674 us -> 435 us (0.65)
  waiting for transfers between devices: 477 us -> 249 us
  blocking collectives: 79.5 us -> 0 us
  local copies, waits for them, and re-layouts: 7.27 us -> 36.3 us
  other arithmetic: 7.89 us -> 31.3 us
  starting transfers between devices: 14.2 us -> 36.5 us
    reduce_scatter x2 -> x0, waiting for transfers between devices: 341 us -> none  [routed_by_gather(): pieces.append(lax.psum_scatter(part, BOTH, scatter_dimension=0, tiled=True))]
    ppermute x0 -> x10, waiting for transfers between devices: none -> 101 us  [halved_sum(): got = lax.ppermute(sent, axis, pairs)]
    all_gather x1 -> x0, blocking collectives: 79.5 us -> none  [local(): lax.all_gather(jnp.concatenate([packed, segment_ids, segment_ids], axis=0...]
    convert_element_type x0 -> x11, other arithmetic: none -> 19.9 us  [the longest x10 19.2 us: halved_sum(): (kept.astype(jnp.float32) + got.astype(jnp.float32)).astype(jnp.bfloat16)]
    dynamic_slice x1 -> x4, local copies, waits for them, and re-layouts: 0.72 us -> 18.1 us  [the longest x2 13.4 us: halved_sum(): kept = lax.dynamic_index_in_dim(block, mine, place, keepdims=False)]
    ppermute x4 -> x6, starting transfers between devices: 12.9 us -> 25.2 us  [hop(): lax.ppermute(block, 'ctx', [(i, i + 2) for i in devices if i + 2 in devic...]
    ppermute x0 -> x10, starting transfers between devices: none -> 10.4 us  [halved_sum(): got = lax.ppermute(sent, axis, pairs)]
    ppermute x4 -> x6, waiting for transfers between devices: 13 us -> 23.2 us  [hop(): lax.ppermute(block, 'ctx', [(i, i + 2) for i in devices if i + 2 in devic...]
  transfers between devices with their start and end apart: 12 -> 24, of which waited for: 7 -> 14; matrix products, arithmetic and copies ran while one was open for 10% -> 25% of each run, Pallas kernels for 0% -> 0%
where the time goes in v2:
time: 435 us; the launch traced here: 434 us
  waiting for transfers between devices  249 us (57%)
  matrix products  59.2 us (14%)
  starting transfers between devices  36.5 us (8%)
  local copies, waits for them, and re-layouts  36.3 us (8%)
  other arithmetic  31.3 us (7%)
  between operations  13.8 us (3%)
  Pallas kernels  8.41 us (2%)
    all_gather x2, waiting for transfers between devices, routed_by_gather(): tokens = lax.all_gather(wide[span], BOTH, axis=0, tiled=True)  123 us
    ppermute x10, waiting for transfers between devices, halved_sum(): got = lax.ppermute(sent, axis, pairs)  101 us
    dot_general x2, matrix products, expert_half(): inner = jnp.dot(tokens, gate_up, preferred_element_type=jnp.float32)  35.9 us
    ppermute x6, starting transfers between devices, hop(): lax.ppermute(block, 'ctx', [(i, i + 2) for i in devices if i + 2 in devic...  25.2 us
    ppermute x6, waiting for transfers between devices, hop(): lax.ppermute(block, 'ctx', [(i, i + 2) for i in devices if i + 2 in devic...  23.2 us
    convert_element_type x10, other arithmetic, halved_sum(): (kept.astype(jnp.float32) + got.astype(jnp.float32)).astype(jnp.bfloat16)  19.2 us
    dot_general x2, matrix products, expert_half(): return jnp.dot(act, down_rows, preferred_element_type=jnp.float32)  18.5 us
    dynamic_slice x2, local copies, waits for them, and re-layouts, halved_sum(): kept = lax.dynamic_index_in_dim(block, mine, place, keepdims=False)  13.4 us
  transfers between devices with their start and end apart: 24, of which 14 were waited for; matrix products, arithmetic and copies ran while one was open for 25% of the time, Pallas kernels for 0%

profile of v2, /device:TPU:0, one launch (start us, length us, event | category | flops | bytes accessed | tf_op | source)
XLA Modules:
  0.0 434.3 jit_solution(14440672884573485924)
XLA Ops:
  6.5 5.2 %collective-permute-start = (s32[1,128]{1,0:T(1,128)}, s32[1,128]{1,0:T(1,128)S(1)}, u32[]{:S(2)}, u32[]{:S(2)}) collective-permute-start(s32[1,128]{1,0:T(1,128)} %param.14), channel_id=1, source_target_pairs={{0,8},{4,12},{8,16},{12,20},{16,24},{20,28},{1,9},{5,13},{9,17},{1... | collective-permute-start | bytes 1544 | tf_op jit(solution)/shard_map/ppermute | solution.py:23
  11.7 4.3 collective-permute-start.4
  16.0 3.5 collective-permute-start.8
  21.3 6.5 %collective-permute-done.4.refs_1_ = bf16[128,2048]{1,0:T(8,128)(2,1)} collective-permute-done((bf16[128,2048]{1,0:T(8,128)(2,1)}, bf16[128,2048]{1,0:T(8,128)(2,1)}, u32[]{:S(2)}, u32[]{:S(2)}) %collective-permute-start.4) | collective-permute-done | bytes 524320 | tf_op jit(solution)/shard_map/ppermute | solution.py:23
  27.9 4.4 %collective-permute-start.5 = (bf16[128,2048]{1,0:T(8,128)(2,1)}, bf16[128,2048]{1,0:T(8,128)(2,1)S(1)}, u32[]{:S(2)}, u32[]{:S(2)}) collective-permute-start(bf16[128,2048]{1,0:T(8,128)(2,1)} %collective-permute-done.4.refs_1_), channel_id=1, source_target_pairs={{0,8},{4,12},{8,16},{12,20},{16,24},{20,28},{1,9},{5,13},{9,17},{1... | collective-permute-start | bytes 1572872 | tf_op jit(solution)/shard_map/ppermute | solution.py:23
  33.6 3.4 collective-permute-start.1
  37.1 2.0 collective-permute-done.8.refs_6_
  39.1 4.4 %collective-permute-start.9 = (bf16[128,2048]{1,0:T(8,128)(2,1)}, bf16[128,2048]{1,0:T(8,128)(2,1)S(1)}, u32[]{:S(2)}, u32[]{:S(2)}) collective-permute-start(bf16[128,2048]{1,0:T(8,128)(2,1)} %collective-permute-done.8.refs_6_), channel_id=1, source_target_pairs={{0,8},{4,12},{8,16},{12,20},{16,24},{20,28},{1,9},{5,13},{9,17},{1... | collective-permute-start | bytes 1572872 | tf_op jit(solution)/shard_map/ppermute | solution.py:23
  43.6 6.7 %collective-permute-done.5.refs_2_ = bf16[128,2048]{1,0:T(8,128)(2,1)S(1)} collective-permute-done((bf16[128,2048]{1,0:T(8,128)(2,1)}, bf16[128,2048]{1,0:T(8,128)(2,1)S(1)}, u32[]{:S(2)}, u32[]{:S(2)}) %collective-permute-start.5) | collective-permute-done | bytes 524320 | tf_op jit(solution)/shard_map/ppermute | solution.py:23
  50.4 1.9 broadcast_select_fusion.1
  52.3 7.9 %collective-permute-done.9.refs_7_ = bf16[128,2048]{1,0:T(8,128)(2,1)S(1)} collective-permute-done((bf16[128,2048]{1,0:T(8,128)(2,1)}, bf16[128,2048]{1,0:T(8,128)(2,1)S(1)}, u32[]{:S(2)}, u32[]{:S(2)}) %collective-permute-start.9) | collective-permute-done | bytes 524320 | tf_op jit(solution)/shard_map/ppermute | solution.py:23
  60.1 1.9 broadcast_select_fusion
  70.2 8.4 %shard_map.109 = bf16[128,2048]{1,0:T(8,128)(2,1)S(1)} custom-call(f32[128,640]{1,0:T(8,128)S(1)} %and_convert_fusion.mask_ref, bf16[128,2048]{1,0:T(8,128)(2,1)S(1)} %bitcast.96, bf16[128,2048]{1,0:T(8,128)(2,1)S(1)} %bitcast.93, bf16[128,2048]{1,0:T(8,128)(2,1)} %collective-permute-done.4.refs_1_, bf16[128,2048]{1,0:T(8,128)(2,1)S(1)} %collective-permute-done.5.refs_2_, ...), custom_call_target="tpu_custom_call" | custom-call | flops 671088640 | bytes 6291456 | tf_op jit(solution)/shard_map/pallas_call | solution.py:66
  78.6 4.8 %multiply_reduce_fusion = (f32[128]{0:T(128)S(1)}, f32[128,2048]{1,0:T(8,128)S(1)}) fusion(bf16[128,2048]{1,0:T(8,128)(2,1)S(1)} %shard_map.109, bf16[2048,2048]{1,0:T(8,128)(2,1)} %param.16, bf16[1,128,2048]{2,1,0:T(8,128)(2,1)S(1)} %copy-done.14), kind=kOutput, calls=%fused_computation.51 | convolution fusion | flops 1075314560 | bytes 10486272 | tf_op jit(solution)/shard_map/dot_general | solution.py:213
  88.2 80.0 %all-gather.5.cloned.1.call-done = bf16[2048,2176]{1,0:T(8,128)(2,1)} async-done(((bf16[64,2176]{1,0:T(8,128)(2,1)}), bf16[2048,2176]{1,0:T(8,128)(2,1)}) %all-gather.5.cloned.1.call-update) | async-done | bytes 8912912 | tf_op jit(solution)/shard_map/all_gather | solution.py:138
  168.2 2.1 convert_reduce_fusion
  170.2 17.9 %fusion.4 = f32[2048,1408]{0,1:T(8,128)S(1)} fusion(bf16[2048,2176]{1,0:T(8,128)(2,1)} %all-gather.5.cloned.1.call-done, bf16[2048,1408]{1,0:T(8,128)(2,1)} %bitcast.100), kind=kOutput, calls=%fused_computation.10 | convolution fusion | flops 12549357568 | bytes 26214400 | tf_op jit(solution)/shard_map/dot_general | solution.py:93
  188.1 9.2 %select_convert_fusion = bf16[2048,2048]{1,0:T(8,128)(2,1)} fusion(f32[2048]{0:T(1024)S(1)} %get-tuple-element.12, pred[2048]{0:T(1024)(128)(4,1)S(1)} %get-tuple-element.11, f32[2048,1408]{0,1:T(8,128)S(1)} %fusion.4, bf16[1,704,2048]{2,1,0:T(8,128)(2,1)S(1)} %copy-done), kind=kOutput, calls=%fused_computation | convolution fusion | flops 5926813696 | bytes 22816768 | tf_op jit(solution)/shard_map/dot_general | solution.py:95
  197.3 6.7 %constant_dynamic-slice_fusion.1 = (bf16[2,2,1,2,2,64,2048]{6,5,4,3,2,1,0:T(8,128)(2,1)}, bf16[2,2,1,2,2,64,2048]{6,5,4,3,2,1,0:T(8,128)(2,1)S(1)}) fusion(bf16[2,2,2,2,2,64,2048]{6,5,4,3,2,1,0:T(8,128)(2,1)} %bitcast.98, s32[]{:T(128)S(6)} %select_n.115, s32[]{:T(128)S(6)} %select_n.116), kind=kLoop, calls=%fused_computation.72 | loop fusion | bytes 16777224 | tf_op jit(solution)/shard_map/jit(dynamic_index_in_dim)/dynamic_slice | solution.py:113
  204.0 2.3 copy.30
  206.6 42.6 %all-gather.3.cloned.1.call-done = bf16[2048,2176]{1,0:T(8,128)(2,1)} async-done(((bf16[64,2176]{1,0:T(8,128)(2,1)}), bf16[2048,2176]{1,0:T(8,128)(2,1)}) %all-gather.3.cloned.1.call-update) | async-done | bytes 8912912 | tf_op jit(solution)/shard_map/all_gather | solution.py:138
  249.2 2.0 convert_reduce_fusion.1
  251.3 18.1 %fusion.6 = f32[2048,1408]{0,1:T(8,128)S(1)} fusion(bf16[2048,2176]{1,0:T(8,128)(2,1)} %all-gather.3.cloned.1.call-done, bf16[2048,1408]{1,0:T(8,128)(2,1)} %bitcast.101), kind=kOutput, calls=%fused_computation.12 | convolution fusion | flops 12549357568 | bytes 26214400 | tf_op jit(solution)/shard_map/dot_general | solution.py:93
  269.4 9.3 %select_convert_fusion.1 = bf16[2048,2048]{1,0:T(8,128)(2,1)} fusion(f32[2048]{0:T(1024)S(1)} %get-tuple-element.10, pred[2048]{0:T(1024)(128)(4,1)S(1)} %get-tuple-element.9, f32[2048,1408]{0,1:T(8,128)S(1)} %fusion.6, bf16[1,704,2048]{2,1,0:T(8,128)(2,1)S(1)} %copy-done), kind=kOutput, calls=%fused_computation.1 | convolution fusion | flops 5926813696 | bytes 22816768 | tf_op jit(solution)/shard_map/dot_general | solution.py:95
  278.6 6.7 %constant_dynamic-slice_fusion.3 = (bf16[2,2,1,2,2,64,2048]{6,5,4,3,2,1,0:T(8,128)(2,1)}, bf16[2,2,1,2,2,64,2048]{6,5,4,3,2,1,0:T(8,128)(2,1)S(1)}) fusion(bf16[2,2,2,2,2,64,2048]{6,5,4,3,2,1,0:T(8,128)(2,1)} %bitcast.97, s32[]{:T(128)S(6)} %select_n.115, s32[]{:T(128)S(6)} %select_n.116), kind=kLoop, calls=%fused_computation.74 | loop fusion | bytes 16777224 | tf_op jit(solution)/shard_map/jit(dynamic_index_in_dim)/dynamic_slice | solution.py:113
  285.4 2.4 copy.31
  288.0 5.5 %fusion = bf16[2,2,2,2,64,2048]{5,4,3,2,0,1:T(8,128)(2,1)S(1)} fusion(bf16[2,2,2,2,64,2048]{5,4,3,2,0,1:T(8,128)(2,1)} %collective-permute-done.17, bf16[2,2,1,2,2,64,2048]{6,5,4,3,2,1,0:T(8,128)(2,1)} %get-tuple-element.15), kind=kLoop, calls=%fused_computation.3 | loop fusion | flops 8388608 | bytes 12582912 | tf_op jit(solution)/shard_map/convert_element_type | solution.py:117
  293.5 1.6 dynamic-slice_bitcast_fusion
  295.1 1.5 collective-permute-start.18
  296.6 4.1 fusion.1
  300.8 1.6 dynamic-slice_bitcast_fusion.1
  303.4 1.3 collective-permute-start.13
  304.7 38.6 %collective-permute-done.18 = bf16[2,2,2,64,2048]{4,3,2,1,0:T(8,128)(2,1)} collective-permute-done((bf16[2,2,2,64,2048]{4,3,2,1,0:T(8,128)(2,1)}, bf16[2,2,2,64,2048]{4,3,2,1,0:T(8,128)(2,1)}, u32[]{:S(2)}, u32[]{:S(2)}) %collective-permute-start.18) | collective-permute-done | bytes 2097184 | tf_op jit(solution)/shard_map/ppermute | solution.py:116
  343.2 3.0 fusion.8
  347.4 1.9 collective-permute-start.19
  349.3 1.9 collective-permute-done.13
  351.2 2.4 fusion.9
  353.6 1.3 copy-done.12
  356.0 1.5 collective-permute-start.14
  357.5 38.1 %collective-permute-done.19 = bf16[2,2,64,2048]{3,2,1,0:T(8,128)(2,1)} collective-permute-done((bf16[2,2,64,2048]{3,2,1,0:T(8,128)(2,1)}, bf16[2,2,64,2048]{3,2,1,0:T(8,128)(2,1)}, u32[]{:S(2)}, u32[]{:S(2)}) %collective-permute-start.19) | collective-permute-done | bytes 1048608 | tf_op jit(solution)/shard_map/ppermute | solution.py:116
  395.6 1.9 fusion.18
  397.6 1.5 collective-permute-start.20
  399.1 1.9 fusion.19
  401.2 9.3 %collective-permute-done.20 = bf16[2,64,2048]{2,1,0:T(8,128)(2,1)S(1)} collective-permute-done((bf16[2,64,2048]{2,1,0:T(8,128)(2,1)S(1)}, bf16[2,64,2048]{2,1,0:T(8,128)(2,1)S(1)}, u32[]{:S(2)}, u32[]{:S(2)}) %collective-permute-start.20) | collective-permute-done | bytes 524320 | tf_op jit(solution)/shard_map/ppermute | solution.py:116
  410.6 1.3 collective-permute-start.21
  411.9 1.8 collective-permute-done.15
  414.7 2.4 collective-permute-done.21
  417.1 9.3 %collective-permute-done.16 = bf16[64,2048]{1,0:T(8,128)(2,1)S(1)} collective-permute-done((bf16[64,2048]{1,0:T(8,128)(2,1)S(1)}, bf16[64,2048]{1,0:T(8,128)(2,1)S(1)}, u32[]{:S(2)}, u32[]{:S(2)}) %collective-permute-start.16) | collective-permute-done | bytes 262176 | tf_op jit(solution)/shard_map/ppermute | solution.py:116
  (93 shorter events, 22.2 us)
Async XLA Ops:
  6.5 181.6 %copy-start = (bf16[1,704,2048]{2,1,0:T(8,128)(2,1)S(1)}, bf16[1,704,2048]{2,1,0:T(8,128)(2,1)}, u32[]{:S(2)}) copy-start(bf16[1,704,2048]{2,1,0:T(8,128)(2,1)} %param.21) | copy-start | bytes 8650756
  6.5 161.6 %all-gather.5.cloned.1.call-start = ((), (), s32[]{:S(2)}) async-start(), calls=%async_computation.1 | async-start | bytes 9191424 | tf_op jit(solution)/shard_map/all_gather | solution.py:138
  6.5 27.1 %collective-permute-start = (s32[1,128]{1,0:T(1,128)}, s32[1,128]{1,0:T(1,128)S(1)}, u32[]{:S(2)}, u32[]{:S(2)}) collective-permute-start(s32[1,128]{1,0:T(1,128)} %param.14), channel_id=1, source_target_pairs={{0,8},{4,12},{8,16},{12,20},{16,24},{20,28},{1,9},{5,13},{9,17},{1... | collective-permute-start | bytes 1544 | tf_op jit(solution)/shard_map/ppermute | solution.py:23
  11.7 16.2 %collective-permute-start.4 = (bf16[128,2048]{1,0:T(8,128)(2,1)}, bf16[128,2048]{1,0:T(8,128)(2,1)}, u32[]{:S(2)}, u32[]{:S(2)}) collective-permute-start(bf16[128,2048]{1,0:T(8,128)(2,1)} %bitcast.92), channel_id=1, source_target_pairs={{0,8},{4,12},{8,16},{12,20},{16,24},{20,28},{1,9},{5,13},{9,17},{1... | collective-permute-start | bytes 1572872 | tf_op jit(solution)/shard_map/ppermute | solution.py:23
  16.0 23.1 %collective-permute-start.8 = (bf16[128,2048]{1,0:T(8,128)(2,1)}, bf16[128,2048]{1,0:T(8,128)(2,1)}, u32[]{:S(2)}, u32[]{:S(2)}) collective-permute-start(bf16[128,2048]{1,0:T(8,128)(2,1)} %bitcast.94), channel_id=1, source_target_pairs={{0,8},{4,12},{8,16},{12,20},{16,24},{20,28},{1,9},{5,13},{9,17},{1... | collective-permute-start | bytes 1572872 | tf_op jit(solution)/shard_map/ppermute | solution.py:23
  27.9 22.5 %collective-permute-start.5 = (bf16[128,2048]{1,0:T(8,128)(2,1)}, bf16[128,2048]{1,0:T(8,128)(2,1)S(1)}, u32[]{:S(2)}, u32[]{:S(2)}) collective-permute-start(bf16[128,2048]{1,0:T(8,128)(2,1)} %collective-permute-done.4.refs_1_), channel_id=1, source_target_pairs={{0,8},{4,12},{8,16},{12,20},{16,24},{20,28},{1,9},{5,13},{9,17},{1... | collective-permute-start | bytes 1572872 | tf_op jit(solution)/shard_map/ppermute | solution.py:23
  33.6 29.2 %collective-permute-start.1 = (s32[1,128]{1,0:T(1,128)S(1)}, s32[1,128]{1,0:T(1,128)S(1)}, u32[]{:S(2)}, u32[]{:S(2)}) collective-permute-start(s32[1,128]{1,0:T(1,128)S(1)} %collective-permute-done), channel_id=1, source_target_pairs={{0,8},{4,12},{8,16},{12,20},{16,24},{20,28},{1,9},{5,13},{9,17},{1... | collective-permute-start | bytes 1544 | tf_op jit(solution)/shard_map/ppermute | solution.py:23
  37.1 27.0 %collective-permute-start.2 = (s32[1,128]{1,0:T(1,128)S(1)}, s32[1,128]{1,0:T(1,128)S(1)}, u32[]{:S(2)}, u32[]{:S(2)}) collective-permute-start(s32[1,128]{1,0:T(1,128)S(1)} %collective-permute-done), channel_id=1, source_target_pairs={{0,4},{4,0},{8,12},{12,8},{16,20},{20,16},{24,28},{28,24},{1,5},{5... | collective-permute-start | bytes 1544 | tf_op jit(solution)/shard_map/ppermute | solution.py:28
  39.1 21.0 %collective-permute-start.9 = (bf16[128,2048]{1,0:T(8,128)(2,1)}, bf16[128,2048]{1,0:T(8,128)(2,1)S(1)}, u32[]{:S(2)}, u32[]{:S(2)}) collective-permute-start(bf16[128,2048]{1,0:T(8,128)(2,1)} %collective-permute-done.8.refs_6_), channel_id=1, source_target_pairs={{0,8},{4,12},{8,16},{12,20},{16,24},{20,28},{1,9},{5,13},{9,17},{1... | collective-permute-start | bytes 1572872 | tf_op jit(solution)/shard_map/ppermute | solution.py:23
  43.6 22.4 %collective-permute-start.6 = (bf16[128,2048]{1,0:T(8,128)(2,1)}, bf16[128,2048]{1,0:T(8,128)(2,1)}, u32[]{:S(2)}, u32[]{:S(2)}) collective-permute-start(bf16[128,2048]{1,0:T(8,128)(2,1)} %collective-permute-done.4.refs_1_), channel_id=1, source_target_pairs={{0,4},{4,0},{8,12},{12,8},{16,20},{20,16},{24,28},{28,24},{1,5},{5... | collective-permute-start | bytes 1572872 | tf_op jit(solution)/shard_map/ppermute | solution.py:28
  50.4 15.6 %collective-permute-start.10 = (bf16[128,2048]{1,0:T(8,128)(2,1)}, bf16[128,2048]{1,0:T(8,128)(2,1)}, u32[]{:S(2)}, u32[]{:S(2)}) collective-permute-start(bf16[128,2048]{1,0:T(8,128)(2,1)} %collective-permute-done.8.refs_6_), channel_id=1, source_target_pairs={{0,4},{4,0},{8,12},{12,8},{16,20},{20,16},{24,28},{28,24},{1,5},{5... | collective-permute-start | bytes 1572872 | tf_op jit(solution)/shard_map/ppermute | solution.py:28
  60.1 5.9 %collective-permute-start.7 = (bf16[128,2048]{1,0:T(8,128)(2,1)}, bf16[128,2048]{1,0:T(8,128)(2,1)}, u32[]{:S(2)}, u32[]{:S(2)}) collective-permute-start(bf16[128,2048]{1,0:T(8,128)(2,1)} %broadcast_select_fusion.1), channel_id=1, source_target_pairs={{0,4},{4,0},{8,12},{12,8},{16,20},{20,16},{24,28},{28,24},{1,5},{5... | collective-permute-start | bytes 1572872 | tf_op jit(solution)/shard_map/ppermute | solution.py:28
  62.0 0.8 copy-start.3
  62.8 3.2 collective-permute-start.11
  64.0 1.1 collective-permute-start.3
  66.0 1.0 copy-start.1
  67.1 1.0 copy-start.2
  68.1 1.0 copy-start.4
  69.1 1.0 copy-start.5
  70.2 8.4 %copy-start.14 = (bf16[1,128,2048]{2,1,0:T(8,128)(2,1)S(1)}, bf16[1,128,2048]{2,1,0:T(8,128)(2,1)}, u32[]{:S(2)}) copy-start(bf16[1,128,2048]{2,1,0:T(8,128)(2,1)} %param.15) | copy-start | bytes 1572868
  78.6 5.8 %copy-start.17 = (f32[2048]{0:T(1024)S(1)}, f32[2048]{0:T(1024)}, u32[]{:S(2)}) copy-start(f32[2048]{0:T(1024)} %param.17) | copy-start | bytes 24580
  78.6 6.8 %copy-start.15 = (bf16[128,6]{1,0:T(8,128)(2,1)S(1)}, bf16[128,6]{1,0:T(8,128)(2,1)}, u32[]{:S(2)}) copy-start(bf16[128,6]{1,0:T(8,128)(2,1)} %get-tuple-element.23) | copy-start | bytes 4612
  78.6 6.8 %copy-start.16 = (bf16[128,6]{1,0:T(8,128)(2,1)S(1)}, bf16[128,6]{1,0:T(8,128)(2,1)}, u32[]{:S(2)}) copy-start(bf16[128,6]{1,0:T(8,128)(2,1)} %get-tuple-element.24) | copy-start | bytes 4612
  83.4 1.0 copy-start.10
  87.4 161.8 %all-gather.3.cloned.1.call-start = ((), (), s32[]{:S(2)}) async-start(), calls=%async_computation | async-start | bytes 9191424 | tf_op jit(solution)/shard_map/all_gather | solution.py:138
  206.4 81.6 %collective-permute-start.17 = (bf16[2,2,2,2,64,2048]{5,4,3,2,0,1:T(8,128)(2,1)}, bf16[2,2,2,2,64,2048]{5,4,3,2,0,1:T(8,128)(2,1)}, u32[]{:S(2)}, u32[]{:S(2)}) collective-permute-start(bf16[2,2,2,2,64,2048]{5,4,3,2,0,1:T(8,128)(2,1)} %bitcast.90), channel_id=1, source_target_pairs={{0,4},{4,0},{8,12},{12,8},{16,20},{20,16},{24,28},{28,24},{1,5},{5... | collective-permute-start | bytes 12582920 | tf_op jit(solution)/shard_map/ppermute | solution.py:116
  287.7 8.9 %collective-permute-start.12 = (bf16[2,2,2,2,64,2048]{5,4,0,1,2,3:T(8,128)(2,1)}, bf16[2,2,2,2,64,2048]{5,4,0,1,2,3:T(8,128)(2,1)}, u32[]{:S(2)}, u32[]{:S(2)}) collective-permute-start(bf16[2,2,2,2,64,2048]{5,4,0,1,2,3:T(8,128)(2,1)} %bitcast.91), channel_id=1, source_target_pairs={{0,4},{4,0},{8,12},{12,8},{16,20},{20,16},{24,28},{28,24},{1,5},{5... | collective-permute-start | bytes 12582920 | tf_op jit(solution)/shard_map/ppermute | solution.py:116
  288.0 8.6 %copy-start.9 = (bf16[2,2,1,2,2,64,2048]{6,5,4,3,2,1,0:T(8,128)(2,1)S(1)}, bf16[2,2,1,2,2,64,2048]{6,5,4,3,2,1,0:T(8,128)(2,1)}, u32[]{:S(2)}) copy-start(bf16[2,2,1,2,2,64,2048]{6,5,4,3,2,1,0:T(8,128)(2,1)} %get-tuple-element.13) | copy-start | bytes 12582916
  293.5 7.2 %copy-start.6 = (bf16[2,2,2,2,64,2048]{5,4,3,2,0,1:T(8,128)(2,1)}, bf16[2,2,2,2,64,2048]{5,4,3,2,0,1:T(8,128)(2,1)S(1)}, u32[]{:S(2)}) copy-start(bf16[2,2,2,2,64,2048]{5,4,3,2,0,1:T(8,128)(2,1)S(1)} %fusion) | copy-start | bytes 12582916
  295.1 48.1 %collective-permute-start.18 = (bf16[2,2,2,64,2048]{4,3,2,1,0:T(8,128)(2,1)}, bf16[2,2,2,64,2048]{4,3,2,1,0:T(8,128)(2,1)}, u32[]{:S(2)}, u32[]{:S(2)}) collective-permute-start(bf16[2,2,2,64,2048]{4,3,2,1,0:T(8,128)(2,1)} %dynamic-slice_bitcast_fusion), channel_id=1, source_target_pairs={{0,8},{4,12},{8,0},{12,4},{16,24},{20,28},{24,16},{28,20},{1,9},{5... | collective-permute-start | bytes 6291464 | tf_op jit(solution)/shard_map/ppermute | solution.py:116
  300.8 2.6 copy-start.7
  303.4 47.8 %collective-permute-start.13 = (bf16[2,2,2,64,2048]{4,3,0,1,2:T(8,128)(2,1)}, bf16[2,2,2,64,2048]{4,3,0,1,2:T(8,128)(2,1)}, u32[]{:S(2)}, u32[]{:S(2)}) collective-permute-start(bf16[2,2,2,64,2048]{4,3,0,1,2:T(8,128)(2,1)} %dynamic-slice_bitcast_fusion.1), channel_id=1, source_target_pairs={{0,1},{1,0},{2,3},{3,2},{4,5},{5,4},{6,7},{7,6},{8,9},{9,8},{10,11... | collective-permute-start | bytes 6291464 | tf_op jit(solution)/shard_map/ppermute | solution.py:116
  304.7 46.6 %copy-start.8 = (bf16[2,2,2,2,64,2048]{5,4,0,1,2,3:T(8,128)(2,1)S(1)}, bf16[2,2,2,2,64,2048]{5,4,0,1,2,3:T(8,128)(2,1)}, u32[]{:S(2)}) copy-start(bf16[2,2,2,2,64,2048]{5,4,0,1,2,3:T(8,128)(2,1)} %copy-done.7) | copy-start | bytes 12582916
  346.2 3.1 copy-start.13
  347.4 48.2 %collective-permute-start.19 = (bf16[2,2,64,2048]{3,2,1,0:T(8,128)(2,1)}, bf16[2,2,64,2048]{3,2,1,0:T(8,128)(2,1)}, u32[]{:S(2)}, u32[]{:S(2)}) collective-permute-start(bf16[2,2,64,2048]{3,2,1,0:T(8,128)(2,1)} %dynamic-slice_bitcast_fusion.2), channel_id=1, source_target_pairs={{0,16},{4,20},{8,24},{12,28},{16,0},{20,4},{24,8},{28,12},{1,17},{... | collective-permute-start | bytes 3145736 | tf_op jit(solution)/shard_map/ppermute | solution.py:116
  353.6 1.3 copy-start.12
  356.0 43.1 %collective-permute-start.14 = (bf16[2,2,64,2048]{3,2,0,1:T(8,128)(2,1)}, bf16[2,2,64,2048]{3,2,0,1:T(8,128)(2,1)}, u32[]{:S(2)}, u32[]{:S(2)}) collective-permute-start(bf16[2,2,64,2048]{3,2,0,1:T(8,128)(2,1)} %dynamic-slice_bitcast_fusion.3), channel_id=1, source_target_pairs={{0,2},{1,3},{2,0},{3,1},{4,6},{5,7},{6,4},{7,5},{8,10},{9,11},{10,... | collective-permute-start | bytes 3145736 | tf_op jit(solution)/shard_map/ppermute | solution.py:116
  397.5 29.0 %copy-start.11 = (f32[128,2048]{1,0:T(8,128)S(1)}, f32[128,2048]{1,0:T(8,128)}, u32[]{:S(2)}) copy-start(f32[128,2048]{1,0:T(8,128)} %copy-done.10) | copy-start | bytes 3145732
  397.6 12.9 %collective-permute-start.20 = (bf16[2,64,2048]{2,1,0:T(8,128)(2,1)S(1)}, bf16[2,64,2048]{2,1,0:T(8,128)(2,1)S(1)}, u32[]{:S(2)}, u32[]{:S(2)}) collective-permute-start(bf16[2,64,2048]{2,1,0:T(8,128)(2,1)S(1)} %dynamic-slice_bitcast_fusion.4), channel_id=1, source_target_pairs={{0,2},{1,3},{2,0},{3,1},{4,6},{5,7},{6,4},{7,5},{8,10},{9,11},{10,... | collective-permute-start | bytes 1572872 | tf_op jit(solution)/shard_map/ppermute | solution.py:116
  401.1 12.6 %collective-permute-start.15 = (bf16[2,64,2048]{2,1,0:T(8,128)(2,1)S(1)}, bf16[2,64,2048]{2,1,0:T(8,128)(2,1)S(1)}, u32[]{:S(2)}, u32[]{:S(2)}) collective-permute-start(bf16[2,64,2048]{2,1,0:T(8,128)(2,1)S(1)} %dynamic-slice_bitcast_fusion.5), channel_id=1, source_target_pairs={{0,8},{4,12},{8,0},{12,4},{16,24},{20,28},{24,16},{28,20},{1,9},{5... | collective-permute-start | bytes 1572872 | tf_op jit(solution)/shard_map/ppermute | solution.py:116
  410.6 6.4 %collective-permute-start.21 = (bf16[64,2048]{1,0:T(8,128)(2,1)S(1)}, bf16[64,2048]{1,0:T(8,128)(2,1)S(1)}, u32[]{:S(2)}, u32[]{:S(2)}) collective-permute-start(bf16[64,2048]{1,0:T(8,128)(2,1)S(1)} %dynamic-slice_bitcast_fusion.6), channel_id=1, source_target_pairs={{0,1},{1,0},{2,3},{3,2},{4,5},{5,4},{6,7},{7,6},{8,9},{9,8},{10,11... | collective-permute-start | bytes 786440 | tf_op jit(solution)/shard_map/ppermute | solution.py:116
  413.9 12.6 %collective-permute-start.16 = (bf16[64,2048]{1,0:T(8,128)(2,1)S(1)}, bf16[64,2048]{1,0:T(8,128)(2,1)S(1)}, u32[]{:S(2)}, u32[]{:S(2)}) collective-permute-start(bf16[64,2048]{1,0:T(8,128)(2,1)S(1)} %dynamic-slice_bitcast_fusion.7), channel_id=1, source_target_pairs={{0,16},{4,20},{8,24},{12,28},{16,0},{20,4},{24,8},{28,12},{1,17},{... | collective-permute-start | bytes 786440 | tf_op jit(solution)/shard_map/ppermute | solution.py:116
Sparse Core Ops, SparseCore 0:
  87.5 80.5 all-gather.4
  171.0 78.1 all-gather.2

commit v3 on v2

--- a/solution.py
+++ b/solution.py
@@ -105,6 +105,7 @@
     left = [
         (axis, bit) for axis in BOTH for bit in reversed(range(sizes[axis].bit_length() - 1))
     ]
+    left.remove(("ctx", 0))
     block = part.reshape((2,) * len(left) + part.shape[1:])
     for axis, bit in order:
         place = left.index((axis, bit))
@@ -130,20 +131,33 @@
     part_rows = rows // CHUNKS
     deep = [("ctx", bit) for bit in range(1, lax.axis_size("ctx").bit_length() - 1)]
     flat = [("exp", bit) for bit in range(lax.axis_size("exp").bit_length() - 1)]
-    core = [("ctx", 0)]
-    orders = [core + flat + deep, core + deep + flat[::-1]]
-    pieces = []
-    for c in range(CHUNKS):
-        span = slice(c * part_rows, (c + 1) * part_rows)
-        tokens = lax.all_gather(wide[span], BOTH, axis=0, tiled=True)
+    orders = [flat + deep, deep + flat[::-1]]
+    exp_size = lax.axis_size("exp")
+    groups = [
+        [i * exp_size + j for i in range(core, lax.axis_size("ctx"), 2) for j in range(exp_size)]
+        for core in range(2)
+    ]
+
+    def shares(tokens):
         named = tokens[:, D : D + TOPK].astype(jnp.int32) == owner // 2
         code = tokens[:, D + TOPK : D + 2 * TOPK].astype(jnp.float32)
         share = jnp.sum(jnp.where(named, code, 0.0), axis=1, keepdims=True) / jnp.sum(
             code, axis=1, keepdims=True
         )
         part = expert_half(tokens, w_wide, w_down)
-        part = jnp.where(share > 0.0, part * share, 0.0).astype(jnp.bfloat16)
-        pieces.append(halved_sum(part.reshape(owners, part_rows, D), orders[c % 2]))
+        return jnp.where(share > 0.0, part * share, 0.0).astype(jnp.bfloat16)
+
+    pieces = []
+    for c in range(CHUNKS):
+        span = slice(c * part_rows, (c + 1) * part_rows)
+        tokens = lax.all_gather(
+            wide[span], BOTH, axis=0, tiled=True, axis_index_groups=groups
+        )
+        others = swap(tokens)
+        mine = shares(tokens).astype(jnp.float32)
+        got = swap(shares(others)).astype(jnp.float32)
+        both = (mine + got).astype(jnp.bfloat16)
+        pieces.append(halved_sum(both.reshape(owners // 2, part_rows, D), orders[c % 2]))
     return jnp.concatenate(pieces, axis=0).astype(jnp.float32)
 
 

time: 435 us -> 446 us (1.025)
  waiting for transfers between devices: 249 us -> 280 us
  local copies, waits for them, and re-layouts: 36.3 us -> 21.7 us
  other arithmetic: 31.3 us -> 20.9 us
    all_gather x2, waiting for transfers between devices: 123 us -> 159 us  [routed_by_gather(): lax.all_gather(wide[span], BOTH, axis=0, tiled=True, axis_index_groups=gr...]
    dynamic_slice x2 -> x1, local copies, waits for them, and re-layouts: 13.4 us -> 1.84 us  [halved_sum(): kept = lax.dynamic_index_in_dim(block, mine, place, keepdims=False)]
    convert_element_type x10 -> x8, other arithmetic: 19.2 us -> 9.46 us  [halved_sum(): (kept.astype(jnp.float32) + got.astype(jnp.float32)).astype(jnp.bfloat16)]
    dot_general x2 -> x4, matrix products: 35.9 us -> 38.8 us  [expert_half(): inner = jnp.dot(tokens, gate_up, preferred_element_type=jnp.float32)]
    ppermute x10 -> x8, waiting for transfers between devices: 101 us -> 99.4 us  [halved_sum(): got = lax.ppermute(sent, axis, pairs)]
    unnamed x41 -> x53, local copies, waits for them, and re-layouts: 10.6 us -> 12.3 us
    dot_general x2 -> x4, matrix products: 18.5 us -> 19.6 us  [expert_half(): return jnp.dot(act, down_rows, preferred_element_type=jnp.float32)]
    ppermute x10 -> x8, starting transfers between devices: 10.4 us -> 10.8 us  [halved_sum(): got = lax.ppermute(sent, axis, pairs)]
  transfers between devices with their start and end apart: 24 -> 26, of which waited for: 14 -> 15; matrix products, arithmetic and copies ran while one was open for 25% -> 20% of each run, Pallas kernels for 0% -> 0%
where the time goes in v3:
time: 446 us; the launch traced here: 445 us
  waiting for transfers between devices  280 us (63%)
  matrix products  63.2 us (14%)
  starting transfers between devices  37.1 us (8%)
  local copies, waits for them, and re-layouts  21.7 us (5%)
  other arithmetic  20.9 us (5%)
  between operations  13.9 us (3%)
  Pallas kernels  8.41 us (2%)
    all_gather x2, waiting for transfers between devices, routed_by_gather(): lax.all_gather(wide[span], BOTH, axis=0, tiled=True, axis_index_groups=gr...  159 us
    ppermute x8, waiting for transfers between devices, halved_sum(): got = lax.ppermute(sent, axis, pairs)  99.4 us
    dot_general x4, matrix products, expert_half(): inner = jnp.dot(tokens, gate_up, preferred_element_type=jnp.float32)  38.8 us
    ppermute x6, starting transfers between devices, hop(): lax.ppermute(block, 'ctx', [(i, i + 2) for i in devices if i + 2 in devic...  24.5 us
    ppermute x6, waiting for transfers between devices, hop(): lax.ppermute(block, 'ctx', [(i, i + 2) for i in devices if i + 2 in devic...  19.7 us
    dot_general x4, matrix products, expert_half(): return jnp.dot(act, down_rows, preferred_element_type=jnp.float32)  19.6 us
    unnamed x53, local copies, waits for them, and re-layouts  12.3 us
    ppermute x8, starting transfers between devices, halved_sum(): got = lax.ppermute(sent, axis, pairs)  10.8 us
  transfers between devices with their start and end apart: 26, of which 15 were waited for; matrix products, arithmetic and copies ran while one was open for 20% of the time, Pallas kernels for 0%

profile of v3, /device:TPU:0, one launch (start us, length us, event | category | flops | bytes accessed | tf_op | source)
XLA Modules:
  0.0 445.1 jit_solution(6415306995660913778)
XLA Ops:
  6.5 6.0 %collective-permute-start.8 = (bf16[128,2048]{1,0:T(8,128)(2,1)}, bf16[128,2048]{1,0:T(8,128)(2,1)}, u32[]{:S(2)}, u32[]{:S(2)}) collective-permute-start(bf16[128,2048]{1,0:T(8,128)(2,1)} %bitcast.97), channel_id=1, source_target_pairs={{0,8},{4,12},{8,16},{12,20},{16,24},{20,28},{1,9},{5,13},{9,17},{1... | collective-permute-start | bytes 1572872 | tf_op jit(solution)/shard_map/ppermute | solution.py:23
  12.6 3.5 collective-permute-start.4
  16.0 2.7 collective-permute-start
  20.6 3.8 collective-permute-done.8.refs_6_
  24.4 4.4 collective-permute-start.9
  30.1 5.5 %collective-permute-done = s32[1,128]{1,0:T(1,128)S(1)} collective-permute-done((s32[1,128]{1,0:T(1,128)}, s32[1,128]{1,0:T(1,128)S(1)}, u32[]{:S(2)}, u32[]{:S(2)}) %collective-permute-start) | collective-permute-done | bytes 544 | tf_op jit(solution)/shard_map/ppermute | solution.py:23
  35.6 4.4 collective-permute-start.1
  40.1 3.5 collective-permute-start.5
  43.9 3.0 collective-permute-done.9.refs_7_
  46.8 1.9 broadcast_select_fusion
  49.5 7.4 %collective-permute-done.5.refs_2_ = bf16[128,2048]{1,0:T(8,128)(2,1)S(1)} collective-permute-done((bf16[128,2048]{1,0:T(8,128)(2,1)}, bf16[128,2048]{1,0:T(8,128)(2,1)S(1)}, u32[]{:S(2)}, u32[]{:S(2)}) %collective-permute-start.5) | collective-permute-done | bytes 524320 | tf_op jit(solution)/shard_map/ppermute | solution.py:23
  56.9 1.9 broadcast_select_fusion.1
  67.0 8.4 %shard_map.109 = bf16[128,2048]{1,0:T(8,128)(2,1)S(1)} custom-call(f32[128,640]{1,0:T(8,128)S(1)} %and_convert_fusion.mask_ref, bf16[128,2048]{1,0:T(8,128)(2,1)S(1)} %bitcast.99, bf16[128,2048]{1,0:T(8,128)(2,1)S(1)} %bitcast.96, bf16[128,2048]{1,0:T(8,128)(2,1)} %collective-permute-done.4.refs_1_, bf16[128,2048]{1,0:T(8,128)(2,1)S(1)} %copy-done.6, ...), custom_call_target="tpu_custom_call" | custom-call | flops 671088640 | bytes 6291456 | tf_op jit(solution)/shard_map/pallas_call | solution.py:66
  75.4 4.8 %multiply_reduce_fusion = (f32[128]{0:T(128)S(1)}, f32[128,2048]{1,0:T(8,128)S(1)}) fusion(bf16[128,2048]{1,0:T(8,128)(2,1)S(1)} %shard_map.109, bf16[2048,2048]{1,0:T(8,128)(2,1)} %param.16, bf16[1,128,2048]{2,1,0:T(8,128)(2,1)S(1)} %copy-done.15), kind=kOutput, calls=%fused_computation.54 | convolution fusion | flops 1075314560 | bytes 10486272 | tf_op jit(solution)/shard_map/dot_general | solution.py:227
  85.0 79.6 %all-gather.3.cloned.1.call-done = bf16[1024,2176]{1,0:T(8,128)(2,1)} async-done(((bf16[64,2176]{1,0:T(8,128)(2,1)}), bf16[1024,2176]{1,0:T(8,128)(2,1)}) %all-gather.3.cloned.1.call-update) | async-done | bytes 4456464 | tf_op jit(solution)/shard_map/all_gather | solution.py:153
  164.6 79.4 %all-gather.5.cloned.1.call-done = bf16[1024,2176]{1,0:T(8,128)(2,1)} async-done(((bf16[64,2176]{1,0:T(8,128)(2,1)}), bf16[1024,2176]{1,0:T(8,128)(2,1)}) %all-gather.5.cloned.1.call-update) | async-done | bytes 4456464 | tf_op jit(solution)/shard_map/all_gather | solution.py:153
  244.0 12.1 %fusion.6 = f32[1024,1408]{1,0:T(8,128)} fusion(bf16[1024,2176]{1,0:T(8,128)(2,1)} %all-gather.3.cloned.1.call-done, bf16[2048,1408]{1,0:T(8,128)(2,1)} %bitcast.106), kind=kOutput, calls=%fused_computation.12 | convolution fusion | flops 6274678784 | bytes 15990784 | tf_op jit(solution)/shard_map/dot_general | solution.py:93
  256.1 1.4 convert_reduce_fusion.3
  257.5 1.4 convert_reduce_fusion.2
  259.0 10.8 %fusion.4 = f32[1024,1408]{1,0:T(8,128)S(1)} fusion(bf16[1024,2176]{1,0:T(8,128)(2,1)} %collective-permute-done.12, bf16[2048,1408]{1,0:T(8,128)(2,1)} %bitcast.107), kind=kOutput, calls=%fused_computation.10 | convolution fusion | flops 6274678784 | bytes 15990784 | tf_op jit(solution)/shard_map/dot_general | solution.py:93
  269.7 4.5 %select_convert_fusion.2 = bf16[1024,2048]{1,0:T(8,128)(2,1)S(1)} fusion(f32[1024]{0:T(1024)S(1)} %get-tuple-element.16, pred[1024]{0:T(1024)(128)(4,1)S(1)} %get-tuple-element.15, bf16[1,704,2048]{2,1,0:T(8,128)(2,1)S(1)} %copy-done, f32[1024,1408]{1,0:T(8,128)S(1)} %fusion.4), kind=kOutput, calls=%fused_computation.4 | convolution fusion | flops 2963406848 | bytes 13374464 | tf_op jit(solution)/shard_map/dot_general | solution.py:95
  274.8 7.1 %fusion = f32[1024,1408]{1,0:T(8,128)S(1)} fusion(bf16[1024,2176]{1,0:T(8,128)(2,1)S(1)} %collective-permute-done.18, bf16[2048,1408]{1,0:T(8,128)(2,1)S(1)} %bitcast.110), kind=kOutput, calls=%fused_computation.6 | convolution fusion | flops 6274678784 | bytes 15990784 | tf_op jit(solution)/shard_map/dot_general | solution.py:93
  282.3 4.3 select_convert_fusion
  287.1 8.8 %fusion.2 = f32[1024,1408]{1,0:T(8,128)} fusion(bf16[1024,2176]{1,0:T(8,128)(2,1)S(1)} %bitcast.104, bf16[2048,1408]{1,0:T(8,128)(2,1)S(1)} %bitcast.111), kind=kOutput, calls=%fused_computation.8 | convolution fusion | flops 6274678784 | bytes 15990784 | tf_op jit(solution)/shard_map/dot_general | solution.py:93
  295.9 6.4 %add_convert_fusion.1 = bf16[1024,2048]{1,0:T(8,128)(2,1)S(1)} fusion(bf16[1024,2048]{1,0:T(8,128)(2,1)S(1)} %collective-permute-done.13, f32[1024]{0:T(1024)S(1)} %get-tuple-element.14, bf16[1,704,2048]{2,1,0:T(8,128)(2,1)S(1)} %copy-done, pred[1024]{0:T(1024)(128)(4,1)S(1)} %get-tuple-element.13, f32[1024,1408]{1,0:T(8,128)} %fusion.6), kind=kOutput, calls=%fused_computation.3 | convolution fusion | flops 2971795456 | bytes 17568768 | tf_op jit(solution)/shard_map/dot_general | solution.py:95
  302.4 1.8 constant_dynamic-slice_fusion.1
  304.2 1.6 copy.25
  305.8 1.3 collective-permute-start.14
  307.0 4.5 %add_convert_fusion = bf16[1024,2048]{1,0:T(8,128)(2,1)S(1)} fusion(bf16[1024,2048]{1,0:T(8,128)(2,1)S(1)} %collective-permute-done.19, f32[1024]{0:T(1024)S(1)} %get-tuple-element.18, bf16[1,704,2048]{2,1,0:T(8,128)(2,1)S(1)} %copy-done, pred[1024]{0:T(1024)(128)(4,1)S(1)} %get-tuple-element.17, f32[1024,1408]{1,0:T(8,128)S(1)} %copy-done.19), kind=kOutput, calls=%fused_computation | convolution fusion | flops 2971795456 | bytes 17568768 | tf_op jit(solution)/shard_map/dot_general | solution.py:95
  311.5 2.0 copy-done.13
  313.5 1.5 dynamic-slice_bitcast_fusion
  315.0 1.5 collective-permute-start.20
  316.5 37.6 %collective-permute-done.14 = bf16[2,2,2,64,2048]{4,3,0,1,2:T(8,128)(2,1)} collective-permute-done((bf16[2,2,2,64,2048]{4,3,0,1,2:T(8,128)(2,1)}, bf16[2,2,2,64,2048]{4,3,0,1,2:T(8,128)(2,1)}, u32[]{:S(2)}, u32[]{:S(2)}) %collective-permute-start.14) | collective-permute-done | bytes 2097184 | tf_op jit(solution)/shard_map/ppermute | solution.py:117
  354.1 3.2 fusion.9
  358.5 1.5 collective-permute-start.15
  360.0 3.1 collective-permute-done.20
  363.1 2.4 fusion.8
  365.4 1.3 copy-done.10
  367.8 2.0 collective-permute-start.21
  369.8 13.8 %collective-permute-done.15 = bf16[2,2,64,2048]{3,2,0,1:T(8,128)(2,1)} collective-permute-done((bf16[2,2,64,2048]{3,2,0,1:T(8,128)(2,1)}, bf16[2,2,64,2048]{3,2,0,1:T(8,128)(2,1)}, u32[]{:S(2)}, u32[]{:S(2)}) %collective-permute-start.15) | collective-permute-done | bytes 1048608 | tf_op jit(solution)/shard_map/ppermute | solution.py:117
  383.6 1.9 fusion.31
  385.6 1.6 collective-permute-start.16
  387.1 29.0 %collective-permute-done.21 = bf16[2,2,64,2048]{3,2,1,0:T(8,128)(2,1)} collective-permute-done((bf16[2,2,64,2048]{3,2,1,0:T(8,128)(2,1)}, bf16[2,2,64,2048]{3,2,1,0:T(8,128)(2,1)}, u32[]{:S(2)}, u32[]{:S(2)}) %collective-permute-start.21) | collective-permute-done | bytes 1048608 | tf_op jit(solution)/shard_map/ppermute | solution.py:117
  416.1 1.6 fusion.30
  417.8 1.6 collective-permute-start.22
  420.0 10.6 %collective-permute-done.22 = bf16[2,64,2048]{2,1,0:T(8,128)(2,1)S(1)} collective-permute-done((bf16[2,64,2048]{2,1,0:T(8,128)(2,1)S(1)}, bf16[2,64,2048]{2,1,0:T(8,128)(2,1)S(1)}, u32[]{:S(2)}, u32[]{:S(2)}) %collective-permute-start.22) | collective-permute-done | bytes 524320 | tf_op jit(solution)/shard_map/ppermute | solution.py:117
  430.8 1.4 collective-permute-start.23
  432.4 4.8 %collective-permute-done.23 = bf16[64,2048]{1,0:T(8,128)(2,1)S(1)} collective-permute-done((bf16[64,2048]{1,0:T(8,128)(2,1)S(1)}, bf16[64,2048]{1,0:T(8,128)(2,1)S(1)}, u32[]{:S(2)}, u32[]{:S(2)}) %collective-permute-start.23) | collective-permute-done | bytes 262176 | tf_op jit(solution)/shard_map/ppermute | solution.py:117
  (114 shorter events, 22.8 us)
Async XLA Ops:
  6.5 263.2 %copy-start = (bf16[1,704,2048]{2,1,0:T(8,128)(2,1)S(1)}, bf16[1,704,2048]{2,1,0:T(8,128)(2,1)}, u32[]{:S(2)}) copy-start(bf16[1,704,2048]{2,1,0:T(8,128)(2,1)} %param.21) | copy-start | bytes 8650756
  6.5 56.3 %copy-start.1 = (bf16[1,128,2048]{2,1,0:T(8,128)(2,1)S(1)}, bf16[1,128,2048]{2,1,0:T(8,128)(2,1)}, u32[]{:S(2)}) copy-start(bf16[1,128,2048]{2,1,0:T(8,128)(2,1)} %param.12) | copy-start | bytes 1572868
  6.5 158.1 %all-gather.3.cloned.1.call-start = ((), (), s32[]{:S(2)}) async-start(), calls=%async_computation | async-start | bytes 4734976 | tf_op jit(solution)/shard_map/all_gather | solution.py:153
  6.5 17.8 %collective-permute-start.8 = (bf16[128,2048]{1,0:T(8,128)(2,1)}, bf16[128,2048]{1,0:T(8,128)(2,1)}, u32[]{:S(2)}, u32[]{:S(2)}) collective-permute-start(bf16[128,2048]{1,0:T(8,128)(2,1)} %bitcast.97), channel_id=1, source_target_pairs={{0,8},{4,12},{8,16},{12,20},{16,24},{20,28},{1,9},{5,13},{9,17},{1... | collective-permute-start | bytes 1572872 | tf_op jit(solution)/shard_map/ppermute | solution.py:23
  12.6 27.5 %collective-permute-start.4 = (bf16[128,2048]{1,0:T(8,128)(2,1)}, bf16[128,2048]{1,0:T(8,128)(2,1)}, u32[]{:S(2)}, u32[]{:S(2)}) collective-permute-start(bf16[128,2048]{1,0:T(8,128)(2,1)} %bitcast.95), channel_id=1, source_target_pairs={{0,8},{4,12},{8,16},{12,20},{16,24},{20,28},{1,9},{5,13},{9,17},{1... | collective-permute-start | bytes 1572872 | tf_op jit(solution)/shard_map/ppermute | solution.py:23
  16.0 19.6 %collective-permute-start = (s32[1,128]{1,0:T(1,128)}, s32[1,128]{1,0:T(1,128)S(1)}, u32[]{:S(2)}, u32[]{:S(2)}) collective-permute-start(s32[1,128]{1,0:T(1,128)} %param.14), channel_id=1, source_target_pairs={{0,8},{4,12},{8,16},{12,20},{16,24},{20,28},{1,9},{5,13},{9,17},{1... | collective-permute-start | bytes 1544 | tf_op jit(solution)/shard_map/ppermute | solution.py:23
  24.4 22.5 %collective-permute-start.9 = (bf16[128,2048]{1,0:T(8,128)(2,1)}, bf16[128,2048]{1,0:T(8,128)(2,1)S(1)}, u32[]{:S(2)}, u32[]{:S(2)}) collective-permute-start(bf16[128,2048]{1,0:T(8,128)(2,1)} %collective-permute-done.8.refs_6_), channel_id=1, source_target_pairs={{0,8},{4,12},{8,16},{12,20},{16,24},{20,28},{1,9},{5,13},{9,17},{1... | collective-permute-start | bytes 1572872 | tf_op jit(solution)/shard_map/ppermute | solution.py:23
  35.6 24.0 %collective-permute-start.1 = (s32[1,128]{1,0:T(1,128)S(1)}, s32[1,128]{1,0:T(1,128)S(1)}, u32[]{:S(2)}, u32[]{:S(2)}) collective-permute-start(s32[1,128]{1,0:T(1,128)S(1)} %collective-permute-done), channel_id=1, source_target_pairs={{0,8},{4,12},{8,16},{12,20},{16,24},{20,28},{1,9},{5,13},{9,17},{1... | collective-permute-start | bytes 1544 | tf_op jit(solution)/shard_map/ppermute | solution.py:23
  40.0 20.8 %collective-permute-start.2 = (s32[1,128]{1,0:T(1,128)S(1)}, s32[1,128]{1,0:T(1,128)S(1)}, u32[]{:S(2)}, u32[]{:S(2)}) collective-permute-start(s32[1,128]{1,0:T(1,128)S(1)} %collective-permute-done), channel_id=1, source_target_pairs={{0,4},{4,0},{8,12},{12,8},{16,20},{20,16},{24,28},{28,24},{1,5},{5... | collective-permute-start | bytes 1544 | tf_op jit(solution)/shard_map/ppermute | solution.py:28
  40.1 16.9 %collective-permute-start.5 = (bf16[128,2048]{1,0:T(8,128)(2,1)}, bf16[128,2048]{1,0:T(8,128)(2,1)S(1)}, u32[]{:S(2)}, u32[]{:S(2)}) collective-permute-start(bf16[128,2048]{1,0:T(8,128)(2,1)} %collective-permute-done.4.refs_1_), channel_id=1, source_target_pairs={{0,8},{4,12},{8,16},{12,20},{16,24},{20,28},{1,9},{5,13},{9,17},{1... | collective-permute-start | bytes 1572872 | tf_op jit(solution)/shard_map/ppermute | solution.py:23
  43.6 19.2 %collective-permute-start.10 = (bf16[128,2048]{1,0:T(8,128)(2,1)}, bf16[128,2048]{1,0:T(8,128)(2,1)}, u32[]{:S(2)}, u32[]{:S(2)}) collective-permute-start(bf16[128,2048]{1,0:T(8,128)(2,1)} %collective-permute-done.8.refs_6_), channel_id=1, source_target_pairs={{0,4},{4,0},{8,12},{12,8},{16,20},{20,16},{24,28},{28,24},{1,5},{5... | collective-permute-start | bytes 1572872 | tf_op jit(solution)/shard_map/ppermute | solution.py:28
  46.8 15.9 %collective-permute-start.6 = (bf16[128,2048]{1,0:T(8,128)(2,1)}, bf16[128,2048]{1,0:T(8,128)(2,1)}, u32[]{:S(2)}, u32[]{:S(2)}) collective-permute-start(bf16[128,2048]{1,0:T(8,128)(2,1)} %collective-permute-done.4.refs_1_), channel_id=1, source_target_pairs={{0,4},{4,0},{8,12},{12,8},{16,20},{20,16},{24,28},{28,24},{1,5},{5... | collective-permute-start | bytes 1572872 | tf_op jit(solution)/shard_map/ppermute | solution.py:28
  56.9 5.8 %collective-permute-start.11 = (bf16[128,2048]{1,0:T(8,128)(2,1)}, bf16[128,2048]{1,0:T(8,128)(2,1)}, u32[]{:S(2)}, u32[]{:S(2)}) collective-permute-start(bf16[128,2048]{1,0:T(8,128)(2,1)} %broadcast_select_fusion), channel_id=1, source_target_pairs={{0,4},{4,0},{8,12},{12,8},{16,20},{20,16},{24,28},{28,24},{1,5},{5... | collective-permute-start | bytes 1572872 | tf_op jit(solution)/shard_map/ppermute | solution.py:28
  59.6 3.2 collective-permute-start.7
  60.8 1.1 collective-permute-start.3
  62.8 1.0 copy-start.2
  63.9 1.0 copy-start.4
  64.9 1.0 copy-start.6
  65.9 1.0 copy-start.7
  67.0 8.4 %copy-start.15 = (bf16[1,128,2048]{2,1,0:T(8,128)(2,1)S(1)}, bf16[1,128,2048]{2,1,0:T(8,128)(2,1)}, u32[]{:S(2)}) copy-start(bf16[1,128,2048]{2,1,0:T(8,128)(2,1)} %param.15) | copy-start | bytes 1572868
  75.4 5.8 %copy-start.18 = (f32[2048]{0:T(1024)S(1)}, f32[2048]{0:T(1024)}, u32[]{:S(2)}) copy-start(f32[2048]{0:T(1024)} %param.17) | copy-start | bytes 24580
  75.4 6.7 %copy-start.16 = (bf16[128,6]{1,0:T(8,128)(2,1)S(1)}, bf16[128,6]{1,0:T(8,128)(2,1)}, u32[]{:S(2)}) copy-start(bf16[128,6]{1,0:T(8,128)(2,1)} %get-tuple-element.29) | copy-start | bytes 4612
  75.4 6.7 %copy-start.17 = (bf16[128,6]{1,0:T(8,128)(2,1)S(1)}, bf16[128,6]{1,0:T(8,128)(2,1)}, u32[]{:S(2)}) copy-start(bf16[128,6]{1,0:T(8,128)(2,1)} %get-tuple-element.30) | copy-start | bytes 4612
  80.2 1.0 copy-start.8
  84.2 159.8 %all-gather.5.cloned.1.call-start = ((), (), s32[]{:S(2)}) async-start(), calls=%async_computation.1 | async-start | bytes 4734976 | tf_op jit(solution)/shard_map/all_gather | solution.py:153
  164.6 92.9 %collective-permute-start.12 = (bf16[1024,2176]{1,0:T(8,128)(2,1)}, bf16[1024,2176]{1,0:T(8,128)(2,1)}, u32[]{:S(2)}, u32[]{:S(2)}) collective-permute-start(bf16[1024,2176]{1,0:T(8,128)(2,1)} %all-gather.3.cloned.1.call-done), channel_id=1, source_target_pairs={{0,4},{4,0},{8,12},{12,8},{16,20},{20,16},{24,28},{28,24},{1,5},{5... | collective-permute-start | bytes 13369352 | tf_op jit(solution)/shard_map/ppermute | solution.py:28
  244.0 30.8 %collective-permute-start.18 = (bf16[1024,2176]{1,0:T(8,128)(2,1)}, bf16[1024,2176]{1,0:T(8,128)(2,1)S(1)}, u32[]{:S(2)}, u32[]{:S(2)}) collective-permute-start(bf16[1024,2176]{1,0:T(8,128)(2,1)} %all-gather.5.cloned.1.call-done), channel_id=1, source_target_pairs={{0,4},{4,0},{8,12},{12,8},{16,20},{20,16},{24,28},{28,24},{1,5},{5... | collective-permute-start | bytes 13369352 | tf_op jit(solution)/shard_map/ppermute | solution.py:28
  244.0 30.8 %slice-start.2 = ((s8[5767168]{0:T(1024)(128)(4,1)}), s8[4194304]{0:T(1024)(128)(4,1)S(1)}, s32[]{:S(2)}) async-start(s8[5767168]{0:T(1024)(128)(4,1)} %bitcast.108), calls=%async_computation.4 | async-start | bytes 8388608
  258.9 15.9 %slice-start.3 = ((s8[5767168]{0:T(1024)(128)(4,1)}), s8[1572864]{0:T(1024)(128)(4,1)S(1)}, s32[]{:S(2)}) async-start(s8[5767168]{0:T(1024)(128)(4,1)} %bitcast.108), calls=%async_computation.5 | async-start | bytes 3145728
  269.7 16.9 %slice-start = ((s8[4456448]{0:T(1024)(128)(4,1)}), s8[4194304]{0:T(1024)(128)(4,1)S(1)}, s32[]{:S(2)}) async-start(s8[4456448]{0:T(1024)(128)(4,1)} %bitcast.103), calls=%async_computation.2 | async-start | bytes 8388608
  274.2 12.4 %slice-start.1 = ((s8[4456448]{0:T(1024)(128)(4,1)}), s8[262144]{0:T(1024)(128)(4,1)S(1)}, s32[]{:S(2)}) async-start(s8[4456448]{0:T(1024)(128)(4,1)} %bitcast.103), calls=%async_computation.3 | async-start | bytes 524288
  274.2 21.7 %collective-permute-start.13 = (bf16[1024,2048]{1,0:T(8,128)(2,1)S(1)}, bf16[1024,2048]{1,0:T(8,128)(2,1)S(1)}, u32[]{:S(2)}, u32[]{:S(2)}) collective-permute-start(bf16[1024,2048]{1,0:T(8,128)(2,1)S(1)} %select_convert_fusion.2), channel_id=1, source_target_pairs={{0,4},{4,0},{8,12},{12,8},{16,20},{20,16},{24,28},{28,24},{1,5},{5... | collective-permute-start | bytes 12582920 | tf_op jit(solution)/shard_map/ppermute | solution.py:28
  286.6 20.5 %collective-permute-start.19 = (bf16[1024,2048]{1,0:T(8,128)(2,1)S(1)}, bf16[1024,2048]{1,0:T(8,128)(2,1)S(1)}, u32[]{:S(2)}, u32[]{:S(2)}) collective-permute-start(bf16[1024,2048]{1,0:T(8,128)(2,1)S(1)} %select_convert_fusion), channel_id=1, source_target_pairs={{0,4},{4,0},{8,12},{12,8},{16,20},{20,16},{24,28},{28,24},{1,5},{5... | collective-permute-start | bytes 12582920 | tf_op jit(solution)/shard_map/ppermute | solution.py:28
  302.4 4.7 %copy-start.19 = (f32[1024,1408]{1,0:T(8,128)S(1)}, f32[1024,1408]{1,0:T(8,128)}, u32[]{:S(2)}) copy-start(f32[1024,1408]{1,0:T(8,128)} %fusion.2) | copy-start | bytes 17301508
  305.8 48.3 %collective-permute-start.14 = (bf16[2,2,2,64,2048]{4,3,0,1,2:T(8,128)(2,1)}, bf16[2,2,2,64,2048]{4,3,0,1,2:T(8,128)(2,1)}, u32[]{:S(2)}, u32[]{:S(2)}) collective-permute-start(bf16[2,2,2,64,2048]{4,3,0,1,2:T(8,128)(2,1)} %bitcast.94), channel_id=1, source_target_pairs={{0,1},{1,0},{2,3},{3,2},{4,5},{5,4},{6,7},{7,6},{8,9},{9,8},{10,11... | collective-permute-start | bytes 6291464 | tf_op jit(solution)/shard_map/ppermute | solution.py:117
  311.5 2.0 copy-start.13
  315.0 48.1 %collective-permute-start.20 = (bf16[2,2,2,64,2048]{4,3,2,1,0:T(8,128)(2,1)}, bf16[2,2,2,64,2048]{4,3,2,1,0:T(8,128)(2,1)}, u32[]{:S(2)}, u32[]{:S(2)}) collective-permute-start(bf16[2,2,2,64,2048]{4,3,2,1,0:T(8,128)(2,1)} %dynamic-slice_bitcast_fusion), channel_id=1, source_target_pairs={{0,8},{4,12},{8,0},{12,4},{16,24},{20,28},{24,16},{28,20},{1,9},{5... | collective-permute-start | bytes 6291464 | tf_op jit(solution)/shard_map/ppermute | solution.py:117
  354.1 9.0 %copy-start.14 = (bf16[1024,2048]{1,0:T(8,128)(2,1)S(1)}, bf16[1024,2048]{1,0:T(8,128)(2,1)}, u32[]{:S(2)}) copy-start(bf16[1024,2048]{1,0:T(8,128)(2,1)} %copy-done.13) | copy-start | bytes 12582916
  357.3 2.7 copy-start.12
  358.5 25.1 %collective-permute-start.15 = (bf16[2,2,64,2048]{3,2,0,1:T(8,128)(2,1)}, bf16[2,2,64,2048]{3,2,0,1:T(8,128)(2,1)}, u32[]{:S(2)}, u32[]{:S(2)}) collective-permute-start(bf16[2,2,64,2048]{3,2,0,1:T(8,128)(2,1)} %dynamic-slice_bitcast_fusion.2), channel_id=1, source_target_pairs={{0,2},{1,3},{2,0},{3,1},{4,6},{5,7},{6,4},{7,5},{8,10},{9,11},{10,... | collective-permute-start | bytes 3145736 | tf_op jit(solution)/shard_map/ppermute | solution.py:117
  365.4 1.4 copy-start.10
  367.8 48.3 %collective-permute-start.21 = (bf16[2,2,64,2048]{3,2,1,0:T(8,128)(2,1)}, bf16[2,2,64,2048]{3,2,1,0:T(8,128)(2,1)}, u32[]{:S(2)}, u32[]{:S(2)}) collective-permute-start(bf16[2,2,64,2048]{3,2,1,0:T(8,128)(2,1)} %dynamic-slice_bitcast_fusion.1), channel_id=1, source_target_pairs={{0,16},{4,20},{8,24},{12,28},{16,0},{20,4},{24,8},{28,12},{1,17},{... | collective-permute-start | bytes 3145736 | tf_op jit(solution)/shard_map/ppermute | solution.py:117
  369.8 46.3 %copy-start.11 = (bf16[2,2,2,64,2048]{4,3,2,1,0:T(8,128)(2,1)S(1)}, bf16[2,2,2,64,2048]{4,3,2,1,0:T(8,128)(2,1)}, u32[]{:S(2)}) copy-start(bf16[2,2,2,64,2048]{4,3,2,1,0:T(8,128)(2,1)} %copy-done.10) | copy-start | bytes 6291460
  385.6 34.2 %collective-permute-start.16 = (bf16[2,64,2048]{2,1,0:T(8,128)(2,1)S(1)}, bf16[2,64,2048]{2,1,0:T(8,128)(2,1)S(1)}, u32[]{:S(2)}, u32[]{:S(2)}) collective-permute-start(bf16[2,64,2048]{2,1,0:T(8,128)(2,1)S(1)} %dynamic-slice_bitcast_fusion.4), channel_id=1, source_target_pairs={{0,8},{4,12},{8,0},{12,4},{16,24},{20,28},{24,16},{28,20},{1,9},{5... | collective-permute-start | bytes 1572872 | tf_op jit(solution)/shard_map/ppermute | solution.py:117
  417.7 19.6 %copy-start.9 = (f32[128,2048]{1,0:T(8,128)S(1)}, f32[128,2048]{1,0:T(8,128)}, u32[]{:S(2)}) copy-start(f32[128,2048]{1,0:T(8,128)} %copy-done.8) | copy-start | bytes 3145732
  417.8 12.9 %collective-permute-start.22 = (bf16[2,64,2048]{2,1,0:T(8,128)(2,1)S(1)}, bf16[2,64,2048]{2,1,0:T(8,128)(2,1)S(1)}, u32[]{:S(2)}, u32[]{:S(2)}) collective-permute-start(bf16[2,64,2048]{2,1,0:T(8,128)(2,1)S(1)} %dynamic-slice_bitcast_fusion.3), channel_id=1, source_target_pairs={{0,2},{1,3},{2,0},{3,1},{4,6},{5,7},{6,4},{7,5},{8,10},{9,11},{10,... | collective-permute-start | bytes 1572872 | tf_op jit(solution)/shard_map/ppermute | solution.py:117
  419.9 12.4 %collective-permute-start.17 = (bf16[64,2048]{1,0:T(8,128)(2,1)S(1)}, bf16[64,2048]{1,0:T(8,128)(2,1)S(1)}, u32[]{:S(2)}, u32[]{:S(2)}) collective-permute-start(bf16[64,2048]{1,0:T(8,128)(2,1)S(1)} %dynamic-slice_bitcast_fusion.6), channel_id=1, source_target_pairs={{0,16},{4,20},{8,24},{12,28},{16,0},{20,4},{24,8},{28,12},{1,17},{... | collective-permute-start | bytes 786440 | tf_op jit(solution)/shard_map/ppermute | solution.py:117
  430.8 6.4 %collective-permute-start.23 = (bf16[64,2048]{1,0:T(8,128)(2,1)S(1)}, bf16[64,2048]{1,0:T(8,128)(2,1)S(1)}, u32[]{:S(2)}, u32[]{:S(2)}) collective-permute-start(bf16[64,2048]{1,0:T(8,128)(2,1)S(1)} %dynamic-slice_bitcast_fusion.5), channel_id=1, source_target_pairs={{0,1},{1,0},{2,3},{3,2},{4,5},{5,4},{6,7},{7,6},{8,9},{9,8},{10,11... | collective-permute-start | bytes 786440 | tf_op jit(solution)/shard_map/ppermute | solution.py:117
  (2 other events, 1.6 us)
Sparse Core Ops, SparseCore 0:
  84.4 80.2 all-gather.2
  167.3 76.6 all-gather.4
